TPU v7x, 32 devices: a whole 2x2x4 slice. The times are simulated.
32 devices in a mesh: seg: 8 (over z, x), tp: 4 (over y, core).
Axes of the slice: x: 2, y: 2, z: 4, core: 2. Of those that a mesh axis runs over, the one named last changes fastest.
Arguments:
- tokens: bfloat16 [2, 8, 240, 768], P(None, 'seg', 'tp'), may hold values from -6 to 6
- mem_tokens: bfloat16 [16, 768], P('tp'), may hold values from -6 to 6
- segno: int32 [2, 8], P(None, 'seg'), may hold values from 0 to 7, as said below
- gains: bfloat16 [2, 3, 768], replicated, may hold values from 0.5 to 1.5
- shifts: bfloat16 [2, 3, 768], replicated, may hold values from -1 to 1
- assoc: bfloat16 [2, 768, 768], replicated, may hold values from -0.4375 to 0.4375
- w_write: bfloat16 [2, 768, 768], P(None, None, 'tp'), may hold values from -0.875 to 0.875
- w_qkv: bfloat16 [2, 768, 2304], P(None, None, 'tp'), may hold values from -0.21875 to 0.21875
- b_query_value: bfloat16 [2, 1536], P(None, 'tp'), may hold values from -2 to 2
- w_out: bfloat16 [2, 768, 768], P(None, 'tp'), may hold values from -0.4375 to 0.4375
- out_bias: bfloat16 [2, 2, 768], replicated, may hold values from -1 to 1
- w_fc: bfloat16 [2, 768, 3072], P(None, None, 'tp'), may hold values from -0.21875 to 0.21875
- b_fc: bfloat16 [2, 3072], P(None, 'tp'), may hold values from -2 to 2
- w_proj: bfloat16 [2, 3072, 768], P(None, 'tp'), may hold values from -0.109375 to 0.109375
- cot_tokens: bfloat16 [2, 8, 240, 768], P(None, 'seg', 'tp'), may hold values from -6 to 6
- cot_memory: bfloat16 [2, 8, 16, 768], P(None, 'seg', 'tp'), may hold values from -6 to 6
Outputs:
- out_tokens: bfloat16 [2, 8, 240, 768], P(None, 'seg', 'tp')
- out_memory: bfloat16 [2, 8, 16, 768], P(None, 'seg', 'tp')
- grad_tokens: float32 [2, 8, 240, 768], P(None, 'seg', 'tp')
- grad_mem_tokens: float32 [16, 768], P(None, ('seg', 'tp'))
- grad_gains: float32 [2, 3, 768], P(None, None, ('seg', 'tp'))
- grad_shifts: float32 [2, 3, 768], P(None, None, ('seg', 'tp'))
- grad_assoc: float32 [2, 768, 768], P(None, None, ('seg', 'tp'))
- grad_write: float32 [2, 768, 768], P(None, 'seg', 'tp')
- grad_qkv: float32 [2, 768, 2304], P(None, 'seg', 'tp')
- grad_query_value: float32 [2, 1536], P(None, ('seg', 'tp'))
- grad_out: float32 [2, 768, 768], P(None, 'tp', 'seg')
- grad_out_bias: float32 [2, 2, 768], P(None, None, ('seg', 'tp'))
- grad_fc: float32 [2, 768, 3072], P(None, 'seg', 'tp')
- grad_b_fc: float32 [2, 3072], P(None, ('seg', 'tp'))
- grad_proj: float32 [2, 3072, 768], P(None, 'tp', 'seg')
Inputs may be any that keep to these rules, and one draw needn't show every extreme that they name: `segno`: 0 at an item's first segment and one more at each later segment of the same micro-batch; in each draw one micro-batch holds a single item of all 8 segments.
All inputs are finite; a program needn't handle non-finite values.
Results may differ from a plain program's by a relative error of at most 0.02.
Values may be sent and summed in bfloat16 or wider, within the bound.
No kernel may reach another device: no remote copies, remote signals or barrier semaphores. Data moves between devices by JAX's collectives and lax.ppermute only.
A program may use at most 512 MiB of HBM per device.

v0:
```python
import jax
import jax.numpy as jnp
from jax import lax
from jax.sharding import PartitionSpec as P

D = 768
HD = 64
FF = 3072
KD = 384
NMEM = 16
LAYERS = 2


def cut_along(x, dim, devices):
    dims = x.shape
    blocks = x.reshape(*dims[:dim], devices, dims[dim] // devices, *dims[dim + 1 :])
    return jnp.moveaxis(blocks, dim, 0)


def sum_at_owner(x, axis, dim):
    devices = lax.axis_size(axis)
    blocks = lax.all_to_all(cut_along(x, dim, devices), axis, 0, 0, tiled=True)
    return jnp.sum(blocks.astype(jnp.float32), axis=0)


def in_one_piece(arrays, axis, dim, along):
    both = jnp.concatenate(arrays, axis=along)
    filled, at, gathered = (sum_at_owner(both, axis, dim), 0, [])
    for a in arrays:
        gathered.append(lax.slice_in_dim(filled, at, at + a.shape[along], axis=along))
        at += a.shape[along]
    return tuple(gathered)


def norm_rows(stream, gain, shift):
    average = jnp.mean(stream, axis=-1, keepdims=True)
    centred = stream - average
    variance = jnp.mean(centred * centred, axis=-1, keepdims=True)
    return centred * lax.rsqrt(variance + 1e-05) * gain + shift


def features(keys_in):
    paired = jnp.concatenate([jax.nn.softplus(keys_in), jax.nn.softplus(-keys_in)], axis=-1)
    return jnp.concatenate(
        [paired * jnp.roll(paired, -offset, axis=-1) for offset in (1, 2, 3)], axis=-1
    )


def to_global(blocks, mem_rows, pieces):
    groups, _, columns = blocks.shape
    halves = blocks.reshape(groups, pieces, -1, columns)
    return jnp.concatenate(
        [
            halves[:, :, :mem_rows].reshape(groups, -1, columns),
            halves[:, :, mem_rows:].reshape(groups, -1, columns),
        ],
        axis=1,
    )


def to_blocks(full, mem_rows, pieces):
    groups, _, columns = full.shape
    memory = full[:, : pieces * mem_rows].reshape(groups, pieces, mem_rows, columns)
    others = full[:, pieces * mem_rows :].reshape(groups, pieces, -1, columns)
    return jnp.concatenate([memory, others], axis=2).reshape(groups, -1, columns)


def spread(own, mem_rows):
    return to_global(lax.all_gather(own, "tp", axis=1, tiled=True), mem_rows, lax.axis_size("tp"))


def collect(full, mem_rows):
    return lax.psum_scatter(
        to_blocks(full, mem_rows, lax.axis_size("tp")).astype(jnp.bfloat16),
        "tp",
        scatter_dimension=1,
        tiled=True,
    ).astype(jnp.float32)


def row_mask(numbers, total_rows):
    own_seg = lax.axis_index("seg")
    segment_of = jnp.arange(total_rows) // NMEM
    return (
        (segment_of[None, :] < own_seg) & (segment_of[None, :] >= own_seg - numbers[:, None])
    ).astype(jnp.float32)


def memory_forward(feat_k, write_vals, numbers):
    gathered = (
        lax.all_gather(feat_k, "seg", axis=1, tiled=True),
        lax.all_gather(write_vals, "seg", axis=1, tiled=True),
    )
    mask_rows = row_mask(numbers, gathered[0].shape[1])
    mask_low = mask_rows.astype(jnp.bfloat16)
    state_a = jnp.einsum(
        "mjp,mjc->mpc",
        gathered[0],
        gathered[1] * mask_low[..., None],
        preferred_element_type=jnp.float32,
    )
    state_z = jnp.einsum("mj,mjp->mp", mask_low, gathered[0], preferred_element_type=jnp.float32)
    return (state_a, state_z, (gathered[0], gathered[1], mask_rows))


def memory_backward(d_state_a, d_state_z, memo):
    gathered_p, gathered_v, mask_rows = memo
    term_p = (
        jnp.einsum(
            "mjc,mpc->mjp",
            gathered_v.astype(jnp.float32),
            d_state_a,
            precision=lax.Precision.HIGHEST,
        )
        + d_state_z[:, None, :]
    )
    term_v = jnp.einsum(
        "mjp,mpc->mjc", gathered_p.astype(jnp.float32), d_state_a, precision=lax.Precision.HIGHEST
    )
    return (
        lax.psum_scatter(mask_rows[..., None] * term_p, "seg", scatter_dimension=1, tiled=True),
        lax.psum_scatter(mask_rows[..., None] * term_v, "seg", scatter_dimension=1, tiled=True),
    )


def attention_parts(att_in, w_qkv, b_qv):
    head_count = b_qv.shape[0] // (2 * HD)
    groups, row_count, _ = att_in.shape
    bias_halves = b_qv.astype(jnp.float32).reshape(head_count, 2, HD)
    bias_full = jnp.stack(
        [bias_halves[:, 0], jnp.zeros_like(bias_halves[:, 0]), bias_halves[:, 1]], axis=1
    ).reshape(-1)
    packed = (
        jnp.einsum("mrd,dc->mrc", att_in, w_qkv, preferred_element_type=jnp.float32) + bias_full
    ).astype(jnp.bfloat16)
    heads = packed.reshape(groups, row_count, head_count, 3, HD)
    queries, keys_head, values = (heads[:, :, :, 0], heads[:, :, :, 1], heads[:, :, :, 2])
    scores = (
        jnp.einsum("mqhd,mkhd->mhqk", queries, keys_head, preferred_element_type=jnp.float32)
        * 0.125
    )
    positions = jnp.arange(row_count)
    scores = jnp.where(positions[:, None] >= positions[None, :], scores, -1e30)
    probs = jax.nn.softmax(scores, axis=-1)
    return (queries, keys_head, values, probs)


def layer_forward(stream, numbers, weights, mem_rows):
    gain_low, shift_low, assoc, w_write, w_qkv, b_qv, w_out, out_bias, w_fc, b_fc, w_proj = weights
    gain = gain_low.astype(jnp.float32)
    shift = shift_low.astype(jnp.float32)
    key_dim = assoc.shape[0] // 2
    normed = norm_rows(stream, gain[0], shift[0]).astype(jnp.bfloat16)
    read_keys = jnp.einsum(
        "mrd,kd->mrk", normed, assoc[:key_dim], preferred_element_type=jnp.float32
    ).astype(jnp.bfloat16)
    paired = spread(jnp.concatenate([normed, read_keys], axis=-1), mem_rows)
    feat_q = features(paired[..., -key_dim:].astype(jnp.float32))
    tail = paired[:, -NMEM:, :-key_dim]
    feat_k = features(
        jnp.einsum("mnd,kd->mnk", tail, assoc[key_dim:], preferred_element_type=jnp.float32)
    ).astype(jnp.bfloat16)
    write_vals = jnp.einsum(
        "mnd,dc->mnc", tail, w_write, preferred_element_type=jnp.float32
    ).astype(jnp.bfloat16)
    state_a, state_z, memo = memory_forward(feat_k, write_vals, numbers)
    numer = jnp.einsum(
        "mrp,mpc->mrc",
        feat_q.astype(jnp.bfloat16),
        state_a.astype(jnp.bfloat16),
        preferred_element_type=jnp.float32,
    )
    denom = jnp.einsum("mrp,mp->mr", feat_q, state_z, precision=lax.Precision.HIGHEST) + 1.0
    read_cols = (numer / denom[..., None]).astype(jnp.bfloat16)
    read_own = lax.all_to_all(
        to_blocks(read_cols, mem_rows, lax.axis_size("tp")),
        "tp",
        split_axis=1,
        concat_axis=2,
        tiled=True,
    )
    mid = stream + read_own.astype(jnp.float32)
    att_in = spread(norm_rows(mid, gain[1], shift[1]).astype(jnp.bfloat16), mem_rows)
    queries, keys_head, values, probs = attention_parts(att_in, w_qkv, b_qv)
    groups, row_count, _ = att_in.shape
    mixed = (
        jnp.einsum(
            "mhqk,mkhd->mqhd",
            probs.astype(jnp.bfloat16),
            values,
            preferred_element_type=jnp.float32,
        )
        .astype(jnp.bfloat16)
        .reshape(groups, row_count, -1)
    )
    att_part = jnp.einsum("mrc,cd->mrd", mixed, w_out, preferred_element_type=jnp.float32)
    after = mid + collect(att_part, mem_rows) + out_bias[0].astype(jnp.float32)
    mlp_in = spread(norm_rows(after, gain[2], shift[2]).astype(jnp.bfloat16), mem_rows)
    hidden = jax.nn.gelu(
        jnp.einsum("mrd,dc->mrc", mlp_in, w_fc, preferred_element_type=jnp.float32)
        + b_fc.astype(jnp.float32),
        approximate=True,
    ).astype(jnp.bfloat16)
    mlp_part = jnp.einsum("mrc,cd->mrd", hidden, w_proj, preferred_element_type=jnp.float32)
    result = after + collect(mlp_part, mem_rows) + out_bias[1].astype(jnp.float32)
    record = (
        stream,
        mid,
        after,
        paired,
        att_in,
        mlp_in,
        feat_k,
        write_vals,
        state_a,
        state_z,
        memo,
    )
    return (result, record)


def layer_backward(d_result, weights, record, mem_rows):
    gain_low, shift_low, assoc, w_write, w_qkv, b_qv, w_out, out_bias, w_fc, b_fc, w_proj = weights
    gain = gain_low.astype(jnp.float32)
    shift = shift_low.astype(jnp.float32)
    stream, mid, after, paired, att_in, mlp_in, feat_k, write_vals, state_a, state_z, memo = record
    key_dim = assoc.shape[0] // 2
    groups, row_count, _ = att_in.shape
    d_mlp = spread(d_result.astype(jnp.bfloat16), mem_rows)
    pre = jnp.einsum("mrd,dc->mrc", mlp_in, w_fc, preferred_element_type=jnp.float32) + b_fc.astype(
        jnp.float32
    )
    hidden_val, gelu_pull = jax.vjp(lambda inner: jax.nn.gelu(inner, approximate=True), pre)
    hidden = hidden_val.astype(jnp.bfloat16)
    g_proj = jnp.einsum("mrc,mrd->cd", hidden, d_mlp, preferred_element_type=jnp.float32)
    d_hidden = jnp.einsum("mrd,cd->mrc", d_mlp, w_proj, preferred_element_type=jnp.float32)
    d_pre = gelu_pull(d_hidden)[0].astype(jnp.bfloat16)
    g_fc = jnp.einsum("mrd,mrc->dc", mlp_in, d_pre, preferred_element_type=jnp.float32)
    g_bfc = jnp.sum(d_pre.astype(jnp.float32), axis=(0, 1))
    d_norm2 = collect(
        jnp.einsum("mrc,dc->mrd", d_pre, w_fc, preferred_element_type=jnp.float32), mem_rows
    )
    _, norm_pull = jax.vjp(norm_rows, after, gain[2], shift[2])
    d_after_norm, g_gain2, g_shift2 = norm_pull(d_norm2)
    d_after = d_result + d_after_norm
    g_bias1 = jnp.sum(d_result, axis=(0, 1))
    d_att = spread(d_after.astype(jnp.bfloat16), mem_rows)
    queries, keys_head, values, probs = attention_parts(att_in, w_qkv, b_qv)
    probs_low = probs.astype(jnp.bfloat16)
    mixed = (
        jnp.einsum("mhqk,mkhd->mqhd", probs_low, values, preferred_element_type=jnp.float32)
        .astype(jnp.bfloat16)
        .reshape(groups, row_count, -1)
    )
    g_out = jnp.einsum("mrc,mrd->cd", mixed, d_att, preferred_element_type=jnp.float32)
    d_mixed = (
        jnp.einsum("mrd,cd->mrc", d_att, w_out, preferred_element_type=jnp.float32)
        .astype(jnp.bfloat16)
        .reshape(groups, row_count, -1, HD)
    )
    d_probs = jnp.einsum("mqhd,mkhd->mhqk", d_mixed, values, preferred_element_type=jnp.float32)
    d_values = jnp.einsum("mhqk,mqhd->mkhd", probs_low, d_mixed, preferred_element_type=jnp.float32)
    d_scores = (probs * (d_probs - jnp.sum(d_probs * probs, axis=-1, keepdims=True))).astype(
        jnp.bfloat16
    )
    d_queries = (
        jnp.einsum("mhqk,mkhd->mqhd", d_scores, keys_head, preferred_element_type=jnp.float32)
        * 0.125
    )
    d_keys = (
        jnp.einsum("mhqk,mqhd->mkhd", d_scores, queries, preferred_element_type=jnp.float32) * 0.125
    )
    d_packed = (
        jnp.stack([d_queries, d_keys, d_values], axis=3)
        .astype(jnp.bfloat16)
        .reshape(groups, row_count, -1)
    )
    g_qkv = jnp.einsum("mrd,mrc->dc", att_in, d_packed, preferred_element_type=jnp.float32)
    bias_sums = jnp.sum(d_packed.astype(jnp.float32), axis=(0, 1)).reshape(-1, 3, HD)
    g_qv = jnp.stack([bias_sums[:, 0], bias_sums[:, 2]], axis=1).reshape(-1)
    d_norm1 = collect(
        jnp.einsum("mrc,dc->mrd", d_packed, w_qkv, preferred_element_type=jnp.float32), mem_rows
    )
    _, norm_pull = jax.vjp(norm_rows, mid, gain[1], shift[1])
    d_mid_norm, g_gain1, g_shift1 = norm_pull(d_norm1)
    d_mid = d_after + d_mid_norm
    g_bias0 = jnp.sum(d_after, axis=(0, 1))
    d_read = to_global(
        lax.all_to_all(
            d_mid.astype(jnp.bfloat16), "tp", split_axis=2, concat_axis=1, tiled=True
        ).astype(d_mid.dtype),
        mem_rows,
        lax.axis_size("tp"),
    )
    read_keys = paired[..., -key_dim:].astype(jnp.float32)
    feat_q, feat_pull = jax.vjp(features, read_keys)
    feat_low = feat_q.astype(jnp.bfloat16)
    state_low = state_a.astype(jnp.bfloat16)
    numer = jnp.einsum("mrp,mpc->mrc", feat_low, state_low, preferred_element_type=jnp.float32)
    denom = jnp.einsum("mrp,mp->mr", feat_q, state_z, precision=lax.Precision.HIGHEST) + 1.0
    d_numer = (d_read / denom[..., None]).astype(jnp.bfloat16)
    d_denom = -jnp.sum(d_read * numer, axis=-1) / (denom * denom)
    d_state_a = jnp.einsum("mrp,mrc->mpc", feat_low, d_numer, preferred_element_type=jnp.float32)
    d_state_z = jnp.einsum("mrp,mr->mp", feat_q, d_denom, precision=lax.Precision.HIGHEST)
    d_feat_q = (
        jnp.einsum("mrc,mpc->mrp", d_numer, state_low, preferred_element_type=jnp.float32)
        + d_denom[..., None] * state_z[:, None, :]
    )
    d_read_keys = feat_pull(d_feat_q)[0]
    d_feat_k, d_vals = memory_backward(d_state_a, d_state_z, memo)
    d_vals_low = d_vals.astype(jnp.bfloat16)
    tail = paired[:, -NMEM:, :-key_dim]
    g_write = jnp.einsum("mnd,mnc->dc", tail, d_vals_low, preferred_element_type=jnp.float32)
    tail_keys = jnp.einsum("mnd,kd->mnk", tail, assoc[key_dim:], preferred_element_type=jnp.float32)
    _, key_pull = jax.vjp(features, tail_keys)
    d_tail_keys = key_pull(d_feat_k)[0]
    g_assoc_write = jnp.einsum(
        "mnk,mnd->kd", d_tail_keys, tail.astype(jnp.float32), precision=lax.Precision.HIGHEST
    )
    d_tail = jnp.einsum(
        "mnk,kd->mnd",
        d_tail_keys,
        assoc[key_dim:].astype(jnp.float32),
        precision=lax.Precision.HIGHEST,
    )
    d_tail = d_tail + jnp.einsum(
        "mnc,dc->mnd", d_vals_low, w_write, preferred_element_type=jnp.float32
    )
    d_full = jnp.concatenate(
        [jnp.zeros((groups, row_count - NMEM, d_tail.shape[-1]), jnp.float32), d_tail], axis=1
    )
    summed = collect(jnp.concatenate([d_full, d_read_keys], axis=-1), mem_rows)
    d_keys_low = summed[..., -key_dim:].astype(jnp.bfloat16)
    own_norm = norm_rows(stream, gain[0], shift[0]).astype(jnp.bfloat16)
    g_assoc_read = jnp.einsum(
        "mrk,mrd->kd", d_keys_low, own_norm, preferred_element_type=jnp.float32
    )
    d_norm0 = summed[..., :-key_dim] + jnp.einsum(
        "mrk,kd->mrd", d_keys_low, assoc[:key_dim], preferred_element_type=jnp.float32
    )
    _, norm_pull = jax.vjp(norm_rows, stream, gain[0], shift[0])
    d_stream_norm, g_gain0, g_shift0 = norm_pull(d_norm0)
    d_stream = d_mid + d_stream_norm
    layer_grads = (
        jnp.stack([g_gain0, g_gain1, g_gain2]),
        jnp.stack([g_shift0, g_shift1, g_shift2]),
        jnp.concatenate([g_assoc_read, g_assoc_write], axis=0),
        g_write,
        g_qkv,
        g_qv,
        g_out,
        jnp.stack([g_bias0, g_bias1]),
        g_fc,
        g_bfc,
        g_proj,
    )
    return (d_stream, layer_grads)


def local(
    tokens,
    mem_tokens,
    segno,
    gains,
    shifts,
    assoc,
    w_write,
    w_qkv,
    b_query_value,
    w_out,
    out_bias,
    w_fc,
    b_fc,
    w_proj,
    cot_tokens,
    cot_memory,
):
    mem_rows = mem_tokens.shape[0]
    groups = tokens.shape[0]
    numbers = segno[:, 0]
    stream = jnp.concatenate(
        [jnp.broadcast_to(mem_tokens, (groups,) + mem_tokens.shape), tokens[:, 0]], axis=1
    ).astype(jnp.float32)
    saved = []
    for layer_id in range(LAYERS):
        weights = tuple(
            (
                weight[layer_id]
                for weight in (
                    gains,
                    shifts,
                    assoc,
                    w_write,
                    w_qkv,
                    b_query_value,
                    w_out,
                    out_bias,
                    w_fc,
                    b_fc,
                    w_proj,
                )
            )
        )
        stream, record = layer_forward(stream, numbers, weights, mem_rows)
        saved.append((weights, record))
    out_memory = stream[:, :mem_rows].astype(jnp.bfloat16)[:, None]
    out_tokens = stream[:, mem_rows:].astype(jnp.bfloat16)[:, None]
    d_stream = jnp.concatenate([cot_memory[:, 0], cot_tokens[:, 0]], axis=1).astype(jnp.float32)
    per_layer = [None] * LAYERS
    for layer_id in reversed(range(LAYERS)):
        weights, record = saved[layer_id]
        d_stream, layer_grads = layer_backward(d_stream, weights, record, mem_rows)
        per_layer[layer_id] = layer_grads
    stacked = [
        jnp.stack([per_layer[layer_id][position] for layer_id in range(LAYERS)])
        for position in range(11)
    ]
    g_gain, g_shift, g_assoc, g_write, g_qkv, g_qv, g_out, g_bias, g_fc, g_bfc, g_proj = stacked
    tp_index = lax.axis_index("tp")
    grad_mem = jnp.sum(d_stream[:, :mem_rows], axis=0)
    mem_full = lax.dynamic_update_slice(
        jnp.zeros((NMEM, D), jnp.float32), grad_mem, (tp_index * mem_rows, 0)
    )
    qv_full = lax.dynamic_update_slice(
        jnp.zeros((LAYERS, 2 * D), jnp.float32), g_qv, (0, tp_index * g_qv.shape[1])
    )
    fc_full = lax.dynamic_update_slice(
        jnp.zeros((LAYERS, FF), jnp.float32), g_bfc, (0, tp_index * g_bfc.shape[1])
    )
    shared = (
        lax.psum_scatter(g_gain.reshape(-1, D), ("seg", "tp"), scatter_dimension=1, tiled=True),
        lax.psum_scatter(g_shift.reshape(-1, D), ("seg", "tp"), scatter_dimension=1, tiled=True),
        lax.psum_scatter(g_assoc.reshape(-1, D), ("seg", "tp"), scatter_dimension=1, tiled=True),
        lax.psum_scatter(g_bias.reshape(-1, D), ("seg", "tp"), scatter_dimension=1, tiled=True),
        lax.psum_scatter(mem_full, ("seg", "tp"), scatter_dimension=1, tiled=True),
        lax.psum_scatter(qv_full, ("seg", "tp"), scatter_dimension=1, tiled=True),
        lax.psum_scatter(fc_full, ("seg", "tp"), scatter_dimension=1, tiled=True),
    )
    inward = (
        lax.psum_scatter(g_qkv, "seg", scatter_dimension=1, tiled=True),
        lax.psum_scatter(g_write, "seg", scatter_dimension=1, tiled=True),
        lax.psum_scatter(g_fc, "seg", scatter_dimension=1, tiled=True),
    )
    outward = in_one_piece((g_out.astype(jnp.bfloat16), g_proj.astype(jnp.bfloat16)), "seg", 2, 1)
    grad_tokens = d_stream[:, mem_rows:][:, None]
    return (
        out_tokens,
        out_memory,
        grad_tokens,
        shared[4],
        shared[0].reshape(LAYERS, 3, -1),
        shared[1].reshape(LAYERS, 3, -1),
        shared[2].reshape(LAYERS, 2 * KD, -1),
        inward[1],
        inward[0],
        shared[5],
        outward[0],
        shared[3].reshape(LAYERS, 2, -1),
        inward[2],
        shared[6],
        outward[1],
    )


def solution(mesh):
    return jax.shard_map(
        local,
        mesh=mesh,
        in_specs=(
            P(None, "seg", "tp", None),
            P("tp", None),
            P(None, "seg"),
            P(),
            P(),
            P(),
            P(None, None, "tp"),
            P(None, None, "tp"),
            P(None, "tp"),
            P(None, "tp", None),
            P(),
            P(None, None, "tp"),
            P(None, "tp"),
            P(None, "tp", None),
            P(None, "seg", "tp", None),
            P(None, "seg", "tp", None),
        ),
        out_specs=(
            P(None, "seg", "tp", None),
            P(None, "seg", "tp", None),
            P(None, "seg", "tp", None),
            P(None, ("seg", "tp")),
            P(None, None, ("seg", "tp")),
            P(None, None, ("seg", "tp")),
            P(None, None, ("seg", "tp")),
            P(None, "seg", "tp"),
            P(None, "seg", "tp"),
            P(None, ("seg", "tp")),
            P(None, "tp", "seg"),
            P(None, None, ("seg", "tp")),
            P(None, "seg", "tp"),
            P(None, ("seg", "tp")),
            P(None, "tp", "seg"),
        ),
        check_vma=False,
    )
```

profile of v0, /device:TPU:0, one launch (start us, length us, event | category | flops | bytes accessed | tf_op | source)
XLA Modules:
  0.0 1776.6 jit_solution(2697816688806697802)
XLA Ops:
  15.2 20.2 %all-gather.5.cloned.1.call-done = bf16[2,256,1152]{2,1,0:T(8,128)(2,1)} async-done(((bf16[2,64,1152]{2,1,0:T(8,128)(2,1)}), bf16[2,256,1152]{2,1,0:T(8,128)(2,1)}) %all-gather.5.cloned.1.call-update) | async-done | bytes 1179664 | tf_op jit(solution)/shard_map/all_gather | solution.py:69
  46.8 31.1 %all_gather.44 = bf16[2,128,192]{2,1,0:T(8,128)(2,1)S(1)} all-gather(bf16[2,16,192]{2,1,0:T(8,128)(2,1)S(1)} %convolution_convert_fusion.17), channel_id=1, replica_groups=mesh['seg'=8,'tp'=4] {'seg'}, dimensions={1}, use_global_device_ids=true | all-gather | bytes 110592 | tf_op jit(solution)/shard_map/all_gather | solution.py:92
  85.8 6.1 fusion.10
  101.3 4.7 all-to-all-done
  107.4 8.4 all_gather.45
  127.4 22.7 %reduce-scatter.30.cloned.1.call-done = bf16[2,64,768]{2,1,0:T(8,128)(2,1)} async-done(((bf16[2,256,768]{2,1,0:T(8,128)(2,1)}), bf16[2,64,768]{2,1,0:T(8,128)(2,1)}) %reduce-scatter.30.cloned.1.call-update) | async-done | bytes 196624 | tf_op jit(solution)/shard_map/reduce_scatter | solution.py:73
  151.6 8.2 all_gather.46
  168.6 23.1 %reduce-scatter.32.cloned.1.call-done = bf16[2,64,768]{2,1,0:T(8,128)(2,1)} async-done(((bf16[2,256,768]{2,1,0:T(8,128)(2,1)}), bf16[2,64,768]{2,1,0:T(8,128)(2,1)}) %reduce-scatter.32.cloned.1.call-update) | async-done | bytes 196624 | tf_op jit(solution)/shard_map/reduce_scatter | solution.py:73
  196.1 17.4 all-gather.9.cloned.1.call-done
  226.1 31.0 %all_gather.49 = bf16[2,128,192]{2,1,0:T(8,128)(2,1)S(1)} all-gather(bf16[2,16,192]{2,1,0:T(8,128)(2,1)S(1)} %convolution_convert_fusion.16), channel_id=1, replica_groups=mesh['seg'=8,'tp'=4] {'seg'}, dimensions={1}, use_global_device_ids=true | all-gather | bytes 110592 | tf_op jit(solution)/shard_map/all_gather | solution.py:92
  264.6 6.5 fusion.7
  281.7 5.1 all-to-all-done.1
  293.0 8.0 all_gather.50
  309.8 3.4 fusion.283
  320.9 8.7 all_gather.52
  337.0 5.4 reduce-scatter.34.cloned.1.call-done
  345.0 8.6 all_gather.51
  362.7 3.9 convert_reduce_fusion.1
  375.8 18.2 %reduce-scatter.38.cloned.1.call-done = bf16[2,64,768]{2,1,0:T(8,128)(2,1)} async-done(((bf16[2,256,768]{2,1,0:T(8,128)(2,1)}), bf16[2,64,768]{2,1,0:T(8,128)(2,1)}) %reduce-scatter.38.cloned.1.call-update) | async-done | bytes 196624 | tf_op jit(solution)/shard_map/reduce_scatter | solution.py:73
  399.5 20.3 %reduce-scatter.36.cloned.1.call-done = bf16[2,64,768]{2,1,0:T(8,128)(2,1)} async-done(((bf16[2,256,768]{2,1,0:T(8,128)(2,1)}), bf16[2,64,768]{2,1,0:T(8,128)(2,1)}) %reduce-scatter.36.cloned.1.call-update) | async-done | bytes 196624 | tf_op jit(solution)/shard_map/reduce_scatter | solution.py:73
  423.3 8.4 all_gather.53
  446.6 23.7 %reduce-scatter.40.cloned.1.call-done = bf16[2,64,768]{2,1,0:T(8,128)(2,1)} async-done(((bf16[2,256,768]{2,1,0:T(8,128)(2,1)}), bf16[2,64,768]{2,1,0:T(8,128)(2,1)}) %reduce-scatter.40.cloned.1.call-update) | async-done | bytes 196624 | tf_op jit(solution)/shard_map/reduce_scatter | solution.py:73
  480.9 9.4 all_to_all.20
  511.8 5.0 fusion.6
  529.1 43.9 %reduce-scatter.44.cloned.1.call-done = f32[2,16,192]{2,1,0:T(8,128)} async-done(((f32[2,128,192]{2,1,0:T(8,128)}), f32[2,16,192]{2,1,0:T(8,128)}) %reduce-scatter.44.cloned.1.call-update) | async-done | bytes 24592 | tf_op jit(solution)/shard_map/reduce_scatter | solution.py:122
  573.9 70.5 %reduce-scatter.42.cloned.1.call-done = f32[2,16,2304]{2,1,0:T(8,128)} async-done(((f32[2,128,2304]{2,1,0:T(8,128)}), f32[2,16,2304]{2,1,0:T(8,128)}) %reduce-scatter.42.cloned.1.call-update) | async-done | bytes 294928 | tf_op jit(solution)/shard_map/reduce_scatter | solution.py:121
  653.0 24.9 %reduce-scatter.46.cloned.1.call-done = bf16[2,64,1152]{2,1,0:T(8,128)(2,1)} async-done(((bf16[2,256,1152]{2,1,0:T(8,128)(2,1)}), bf16[2,64,1152]{2,1,0:T(8,128)(2,1)}) %reduce-scatter.46.cloned.1.call-update) | async-done | bytes 294928 | tf_op jit(solution)/shard_map/reduce_scatter | solution.py:73
  681.8 8.6 all_gather.54
  692.8 3.8 convert_reduce_fusion.2
  700.2 23.8 %reduce-scatter.48.cloned.1.call-done = bf16[2,64,768]{2,1,0:T(8,128)(2,1)} async-done(((bf16[2,256,768]{2,1,0:T(8,128)(2,1)}), bf16[2,64,768]{2,1,0:T(8,128)(2,1)}) %reduce-scatter.48.cloned.1.call-update) | async-done | bytes 196624 | tf_op jit(solution)/shard_map/reduce_scatter | solution.py:73
  729.3 8.2 all_gather.55
  747.9 23.6 %reduce-scatter.50.cloned.1.call-done = bf16[2,64,768]{2,1,0:T(8,128)(2,1)} async-done(((bf16[2,256,768]{2,1,0:T(8,128)(2,1)}), bf16[2,64,768]{2,1,0:T(8,128)(2,1)}) %reduce-scatter.50.cloned.1.call-update) | async-done | bytes 196624 | tf_op jit(solution)/shard_map/reduce_scatter | solution.py:73
  777.0 7.7 all_to_all.42
  802.3 4.5 fusion.9
  819.9 43.7 %reduce-scatter.54.cloned.1.call-done = f32[2,16,192]{2,1,0:T(8,128)} async-done(((f32[2,128,192]{2,1,0:T(8,128)}), f32[2,16,192]{2,1,0:T(8,128)}) %reduce-scatter.54.cloned.1.call-update) | async-done | bytes 24592 | tf_op jit(solution)/shard_map/reduce_scatter | solution.py:122
  864.6 70.9 %reduce-scatter.52.cloned.1.call-done = f32[2,16,2304]{2,1,0:T(8,128)} async-done(((f32[2,128,2304]{2,1,0:T(8,128)}), f32[2,16,2304]{2,1,0:T(8,128)}) %reduce-scatter.52.cloned.1.call-update) | async-done | bytes 294928 | tf_op jit(solution)/shard_map/reduce_scatter | solution.py:121
  951.0 4.1 pad_maximum_fusion.4
  955.1 7.4 copy.487
  982.4 5.0 pad_maximum_fusion.2
  987.3 6.1 copy.486
  1013.0 4.6 all-to-all-start.4
  1020.4 90.8 %reduce-scatter.66.cloned.1.call-done = f32[96,2]{1,0:T(8,128)} async-done(((f32[3072,2]{1,0:T(8,128)}), f32[96,2]{1,0:T(8,128)}) %reduce-scatter.66.cloned.1.call-update) | async-done | bytes 784
  1112.6 98.1 %reduce-scatter.64.cloned.1.call-done = f32[48,2]{1,0:T(8,128)} async-done(((f32[1536,2]{1,0:T(8,128)}), f32[48,2]{1,0:T(8,128)}) %reduce-scatter.64.cloned.1.call-update) | async-done | bytes 400
  1212.1 150.7 %all-reduce.35.cloned.1.call-done = f32[2,768,576]{2,0,1:T(2,128)} async-done(((f32[2,768,576]{2,0,1:T(2,128)}), f32[2,768,576]{2,0,1:T(2,128)}) %all-reduce.35.cloned.1.call-update) | async-done | bytes 3538960
  1364.7 64.7 %reduce-scatter.62.cloned.1.call-done = f32[96,384]{1,0:T(8,128)} async-done(((f32[768,384]{1,0:T(8,128)}), f32[96,384]{1,0:T(8,128)}) %reduce-scatter.62.cloned.1.call-update) | async-done | bytes 147472
  1436.7 120.3 %all-reduce.37.cloned.1.call-done = (f32[16,768]{1,0:T(8,128)}, f32[6,768]{1,0:T(8,128)}, f32[6,768]{1,0:T(8,128)}, f32[4,768]{1,0:T(4,128)}) async-done(((f32[16,768]{1,0:T(8,128)}, f32[6,768]{1,0:T(8,128)}, f32[6,768]{1,0:T(8,128)}, f32[4,768]{1,0:T(4,128)}), (f32[16,768]{1,0:T(8,128)}, f32[6,768]{1,0:T(8,128)}, f32[6,768]{1,0:T(8,128)}, f32[4,768]{1,0:T(4,128)})) %all-reduce.37.cloned.1.call-update) | async-done | bytes 98320
  1562.5 107.9 %reduce-scatter.58.cloned.1.call-done = f32[1536,24]{0,1:T(8,128)} async-done(((f32[1536,768]{0,1:T(8,128)}), f32[1536,24]{0,1:T(8,128)}) %reduce-scatter.58.cloned.1.call-update) | async-done | bytes 147472 | tf_op jit(solution)/shard_map/reduce_scatter | solution.py:433
  1672.0 97.5 %reduce-scatter.60.cloned.1.call-done = f32[2,96,768]{2,1,0:T(8,128)} async-done(((f32[2,768,768]{2,1,0:T(8,128)}), f32[2,96,768]{2,1,0:T(8,128)}) %reduce-scatter.60.cloned.1.call-update) | async-done | bytes 589840 | tf_op jit(solution)/shard_map/reduce_scatter | solution.py:442
  (1040 shorter events, 358.1 us)
Async XLA Ops:
  7.2 28.3 %all-gather.5.cloned.1.call-start = ((), (), s32[]{:S(2)}) async-start(), calls=%async_computation.24 | async-start | bytes 1474560 | tf_op jit(solution)/shard_map/all_gather | solution.py:69
  11.0 96.3 %copy-start.27 = (bf16[2,1,60,768]{3,2,0,1:T(8,128)(2,1)}, bf16[2,1,60,768]{3,2,0,1:T(8,128)(2,1)S(1)}, u32[]{:S(2)}) copy-start(bf16[2,1,60,768]{3,2,0,1:T(8,128)(2,1)S(1)} %copy.623) | copy-start | bytes 552964
  11.7 95.5 %copy-start.118 = (bf16[2,4,768]{2,1,0:T(4,128)(2,1)}, bf16[2,4,768]{2,1,0:T(4,128)(2,1)S(1)}, u32[]{:S(2)}) copy-start(bf16[2,4,768]{2,1,0:T(4,128)(2,1)S(1)} %broadcast_in_dim.58) | copy-start | bytes 36868
  15.1 68.5 %all-gather.7.cloned.1.call-start = ((), (), s32[]{:S(2)}) async-start(), calls=%async_computation.25 | async-start | bytes 1327104 | tf_op jit(solution)/shard_map/all_gather | solution.py:91
  96.5 9.4 all-to-all-start
  100.0 50.1 %reduce-scatter.30.cloned.1.call-start = ((), (), s32[]{:S(2)}) async-start(), calls=%async_computation.26 | async-start | bytes 983040 | tf_op jit(solution)/shard_map/reduce_scatter | solution.py:73
  126.1 65.6 %reduce-scatter.32.cloned.1.call-start = ((), (), s32[]{:S(2)}) async-start(), calls=%async_computation.27 | async-start | bytes 983040 | tf_op jit(solution)/shard_map/reduce_scatter | solution.py:73
  167.9 45.6 %all-gather.9.cloned.1.call-start = ((), (), s32[]{:S(2)}) async-start(), calls=%async_computation.28 | async-start | bytes 1474560 | tf_op jit(solution)/shard_map/all_gather | solution.py:69
  195.9 67.1 %all-gather.11.cloned.1.call-start = ((), (), s32[]{:S(2)}) async-start(), calls=%async_computation.29 | async-start | bytes 1327104 | tf_op jit(solution)/shard_map/all_gather | solution.py:91
  277.4 9.4 all-to-all-start.1
  280.8 61.6 %reduce-scatter.34.cloned.1.call-start = ((), (), s32[]{:S(2)}) async-start(), calls=%async_computation.30 | async-start | bytes 983040 | tf_op jit(solution)/shard_map/reduce_scatter | solution.py:73
  318.5 75.5 %reduce-scatter.38.cloned.1.call-start = ((), (), s32[]{:S(2)}) async-start(), calls=%async_computation.32 | async-start | bytes 983040 | tf_op jit(solution)/shard_map/reduce_scatter | solution.py:73
  370.2 49.7 %reduce-scatter.36.cloned.1.call-start = ((), (), s32[]{:S(2)}) async-start(), calls=%async_computation.31 | async-start | bytes 983040 | tf_op jit(solution)/shard_map/reduce_scatter | solution.py:73
  375.7 94.6 %reduce-scatter.40.cloned.1.call-start = ((), (), s32[]{:S(2)}) async-start(), calls=%async_computation.33 | async-start | bytes 983040 | tf_op jit(solution)/shard_map/reduce_scatter | solution.py:73
  446.5 126.5 %reduce-scatter.44.cloned.1.call-start = ((), (), s32[]{:S(2)}) async-start(), calls=%async_computation.35 | async-start | bytes 294912 | tf_op jit(solution)/shard_map/reduce_scatter | solution.py:122
  511.5 132.9 %reduce-scatter.42.cloned.1.call-start = ((), (), s32[]{:S(2)}) async-start(), calls=%async_computation.34 | async-start | bytes 2654208 | tf_op jit(solution)/shard_map/reduce_scatter | solution.py:121
  520.1 157.8 %reduce-scatter.46.cloned.1.call-start = ((), (), s32[]{:S(2)}) async-start(), calls=%async_computation.36 | async-start | bytes 1474560 | tf_op jit(solution)/shard_map/reduce_scatter | solution.py:73
  527.7 116.7 %copy-start.82 = (f32[2,16,384]{2,1,0:T(8,128)S(1)}, f32[2,16,384]{2,1,0:T(8,128)}, u32[]{:S(2)}) copy-start(f32[2,16,384]{2,1,0:T(8,128)} %copy-done.81) | copy-start | bytes 147460
  527.7 116.7 %copy-start.88 = (f32[2,16,384]{2,1,0:T(8,128)S(1)}, f32[2,16,384]{2,1,0:T(8,128)}, u32[]{:S(2)}) copy-start(f32[2,16,384]{2,1,0:T(8,128)} %copy-done.87) | copy-start | bytes 147460
  527.7 118.0 %copy-start.107 = (f32[2,16,766]{2,1,0:T(8,128)S(1)}, f32[2,16,766]{2,1,0:T(8,128)}, u32[]{:S(2)}) copy-start(f32[2,16,766]{2,1,0:T(8,128)} %copy-done.106) | copy-start | bytes 294148
  527.7 118.0 %copy-start.109 = (f32[2,16,765]{2,1,0:T(8,128)S(1)}, f32[2,16,765]{2,1,0:T(8,128)}, u32[]{:S(2)}) copy-start(f32[2,16,765]{2,1,0:T(8,128)} %copy-done.108) | copy-start | bytes 293764
  527.7 118.0 %copy-start.111 = (f32[2,16,767]{2,1,0:T(8,128)S(1)}, f32[2,16,767]{2,1,0:T(8,128)}, u32[]{:S(2)}) copy-start(f32[2,16,767]{2,1,0:T(8,128)} %copy-done.110) | copy-start | bytes 294532
  527.7 118.0 %copy-start.144 = (f32[2,16,3]{2,1,0:T(8,128)S(1)}, f32[2,16,3]{2,1,0:T(8,128)}, u32[]{:S(2)}) copy-start(f32[2,16,3]{2,1,0:T(8,128)} %copy-done.143) | copy-start | bytes 1156
  527.7 118.0 %copy-start.146 = (f32[2,16,2]{2,1,0:T(8,128)S(1)}, f32[2,16,2]{2,1,0:T(8,128)}, u32[]{:S(2)}) copy-start(f32[2,16,2]{2,1,0:T(8,128)} %copy-done.145) | copy-start | bytes 772
  527.7 118.0 %copy-start.148 = (f32[2,16,1]{2,1,0:T(8,128)S(1)}, f32[2,16,1]{2,1,0:T(8,128)}, u32[]{:S(2)}) copy-start(f32[2,16,1]{2,1,0:T(8,128)} %copy-done.147) | copy-start | bytes 388
  529.1 118.4 %copy-start.162 = (f32[2,16,384]{2,1,0:T(8,128)S(1)}, f32[2,16,384]{2,1,0:T(8,128)}, u32[]{:S(2)}) copy-start(f32[2,16,384]{2,1,0:T(8,128)} %get-tuple-element.256) | copy-start | bytes 147460
  653.0 71.0 %reduce-scatter.48.cloned.1.call-start = ((), (), s32[]{:S(2)}) async-start(), calls=%async_computation.37 | async-start | bytes 983040 | tf_op jit(solution)/shard_map/reduce_scatter | solution.py:73
  700.2 71.3 %reduce-scatter.50.cloned.1.call-start = ((), (), s32[]{:S(2)}) async-start(), calls=%async_computation.38 | async-start | bytes 983040 | tf_op jit(solution)/shard_map/reduce_scatter | solution.py:73
  747.7 116.0 %reduce-scatter.54.cloned.1.call-start = ((), (), s32[]{:S(2)}) async-start(), calls=%async_computation.40 | async-start | bytes 294912 | tf_op jit(solution)/shard_map/reduce_scatter | solution.py:122
  802.2 133.3 %reduce-scatter.52.cloned.1.call-start = ((), (), s32[]{:S(2)}) async-start(), calls=%async_computation.39 | async-start | bytes 2654208 | tf_op jit(solution)/shard_map/reduce_scatter | solution.py:121
  810.1 165.6 %reduce-scatter.56.cloned.1.call-start = ((), (), s32[]{:S(2)}) async-start(), calls=%async_computation.41 | async-start | bytes 1474560 | tf_op jit(solution)/shard_map/reduce_scatter | solution.py:73
  818.5 117.0 %copy-start.80 = (f32[2,16,384]{2,1,0:T(8,128)S(1)}, f32[2,16,384]{2,1,0:T(8,128)}, u32[]{:S(2)}) copy-start(f32[2,16,384]{2,1,0:T(8,128)} %copy-done.79) | copy-start | bytes 147460
  818.5 117.0 %copy-start.86 = (f32[2,16,384]{2,1,0:T(8,128)S(1)}, f32[2,16,384]{2,1,0:T(8,128)}, u32[]{:S(2)}) copy-start(f32[2,16,384]{2,1,0:T(8,128)} %copy-done.85) | copy-start | bytes 147460
  818.5 118.2 %copy-start.101 = (f32[2,16,766]{2,1,0:T(8,128)S(1)}, f32[2,16,766]{2,1,0:T(8,128)}, u32[]{:S(2)}) copy-start(f32[2,16,766]{2,1,0:T(8,128)} %copy-done.100) | copy-start | bytes 294148
  818.5 118.2 %copy-start.103 = (f32[2,16,765]{2,1,0:T(8,128)S(1)}, f32[2,16,765]{2,1,0:T(8,128)}, u32[]{:S(2)}) copy-start(f32[2,16,765]{2,1,0:T(8,128)} %copy-done.102) | copy-start | bytes 293764
  818.5 118.2 %copy-start.105 = (f32[2,16,767]{2,1,0:T(8,128)S(1)}, f32[2,16,767]{2,1,0:T(8,128)}, u32[]{:S(2)}) copy-start(f32[2,16,767]{2,1,0:T(8,128)} %copy-done.104) | copy-start | bytes 294532
  818.6 118.2 %copy-start.138 = (f32[2,16,3]{2,1,0:T(8,128)S(1)}, f32[2,16,3]{2,1,0:T(8,128)}, u32[]{:S(2)}) copy-start(f32[2,16,3]{2,1,0:T(8,128)} %copy-done.137) | copy-start | bytes 1156
  818.6 118.2 %copy-start.140 = (f32[2,16,2]{2,1,0:T(8,128)S(1)}, f32[2,16,2]{2,1,0:T(8,128)}, u32[]{:S(2)}) copy-start(f32[2,16,2]{2,1,0:T(8,128)} %copy-done.139) | copy-start | bytes 772
  818.6 118.2 %copy-start.142 = (f32[2,16,1]{2,1,0:T(8,128)S(1)}, f32[2,16,1]{2,1,0:T(8,128)}, u32[]{:S(2)}) copy-start(f32[2,16,1]{2,1,0:T(8,128)} %copy-done.141) | copy-start | bytes 388
  819.9 118.0 %copy-start.160 = (f32[2,16,384]{2,1,0:T(8,128)S(1)}, f32[2,16,384]{2,1,0:T(8,128)}, u32[]{:S(2)}) copy-start(f32[2,16,384]{2,1,0:T(8,128)} %get-tuple-element.251) | copy-start | bytes 147460
  943.4 167.8 %reduce-scatter.66.cloned.1.call-start = ((), (), s32[]{:S(2)}) async-start(), calls=%async_computation.46 | async-start | bytes 1622016
  947.6 263.1 %reduce-scatter.64.cloned.1.call-start = ((), (), s32[]{:S(2)}) async-start(), calls=%async_computation.45 | async-start | bytes 811008
  950.9 411.8 %all-reduce.35.cloned.1.call-start = ((), (), s32[]{:S(2)}) async-start(), calls=%async_computation.47 | async-start | bytes 7864320
  962.6 466.8 %reduce-scatter.62.cloned.1.call-start = ((), (), s32[]{:S(2)}) async-start(), calls=%async_computation.44 | async-start | bytes 1327104
  973.3 583.8 %all-reduce.37.cloned.1.call-start = ((), (), s32[]{:S(2)}) async-start(), calls=%async_computation.48 | async-start | bytes 221184
  982.3 688.1 %reduce-scatter.58.cloned.1.call-start = ((), (), s32[]{:S(2)}) async-start(), calls=%async_computation.42 | async-start | bytes 4866048 | tf_op jit(solution)/shard_map/reduce_scatter | solution.py:433
  993.5 776.0 %reduce-scatter.60.cloned.1.call-start = ((), (), s32[]{:S(2)}) async-start(), calls=%async_computation.43 | async-start | bytes 5308416 | tf_op jit(solution)/shard_map/reduce_scatter | solution.py:442
  1013.0 418.1 %all-to-all-start.4 = ((bf16[8,2,960,96]{2,3,1,0:T(8,128)(2,1)}), bf16[8,2,960,96]{2,3,1,0:T(8,128)(2,1)}, u32[]{:S(2)}, u32[]{:S(2)}) async-start(bf16[8,2,960,96]{2,3,1,0:T(8,128)(2,1)} %maximum_bitcast_fusion), calls=%async_computation.19 | async-start | bytes 6291456 | tf_op jit(solution)/shard_map/all_to_all | solution.py:22
  (241 other events, 1865.5 us)
Sparse Core Ops, SparseCore 0:
  15.2 20.1 all-gather.4
  42.0 41.3 all-gather.6
  126.3 23.7 reduce-scatter.29
  168.0 23.6 reduce-scatter.31
  196.0 17.4 all-gather.8
  221.5 41.4 all-gather.10
  318.6 23.7 reduce-scatter.33
  370.3 23.6 reduce-scatter.37
  396.5 23.2 reduce-scatter.35
  446.6 23.6 reduce-scatter.39
  511.7 61.2 reduce-scatter.43
  576.4 68.0 reduce-scatter.41
  653.1 24.7 reduce-scatter.45
  700.3 23.6 reduce-scatter.47
  747.8 23.6 reduce-scatter.49
  802.3 61.2 reduce-scatter.53
  867.4 68.0 reduce-scatter.51
  943.5 24.7 reduce-scatter.55
  973.6 137.5 reduce-scatter.65
  1116.1 94.5 reduce-scatter.63
  1214.3 148.4 all-reduce.34
  1366.2 63.1 reduce-scatter.61
  1436.0 120.9 all-reduce.36
  1562.4 107.9 reduce-scatter.57
  1675.1 94.3 reduce-scatter.59
where the time goes:
time: 1790 us; the launch traced here: 1780 us
  waiting for transfers between devices  1190 us (66%)
  local copies, waits for them, and re-layouts  163 us (9%)
  blocking collectives  146 us (8%)
  matrix products  131 us (7%)
  other arithmetic  110 us (6%)
  between operations  19.7 us (1%)
    unnamed x30, waiting for transfers between devices  525 us
    reduce_scatter x10, waiting for transfers between devices, collect(): lax.psum_scatter(to_blocks(full, mem_rows, lax.axis_size('tp')).astype(jn...  186 us
    reduce_scatter x2, waiting for transfers between devices, memory_backward(): lax.psum_scatter(mask_rows[..., None] * term_p, 'seg', scatter_dimension=...  141 us
    reduce_scatter x1, waiting for transfers between devices, local(): lax.psum_scatter(g_assoc.reshape(-1, D), ('seg', 'tp'), scatter_dimension...  108 us
    reduce_scatter x1, waiting for transfers between devices, local(): lax.psum_scatter(g_fc, 'seg', scatter_dimension=1, tiled=True)  97.5 us
    reduce_scatter x2, waiting for transfers between devices, memory_backward(): lax.psum_scatter(mask_rows[..., None] * term_v, 'seg', scatter_dimension=...  87.6 us
    unnamed x567, local copies, waits for them, and re-layouts  73 us
    all_gather x8, blocking collectives, spread(): lax.all_gather(own, 'tp', axis=1, tiled=True)  67.2 us
  transfers between devices with their start and end apart: 28, of which 24 were waited for; matrix products, arithmetic and copies ran while one was open for 9% of the time, Pallas kernels for 0%

commit v1 on v0

v1 whole, which is shorter than its diff:
```python
import functools

import jax
import jax.numpy as jnp
from jax import lax
from jax.experimental import pallas as pl
from jax.experimental.pallas import tpu as pltpu
from jax.sharding import PartitionSpec as P

D = 768
HD = 64
NMEM = 16
LAYERS = 2
BF = jnp.bfloat16
F32 = jnp.float32
KERNELS = True


def value_of(item):
    return item[0][item[1]] if isinstance(item, tuple) else item


def phase(body, outs, *items):
    if not KERNELS:
        return body(*[value_of(item) for item in items])
    arrays, specs = [], []
    for item in items:
        if isinstance(item, tuple):
            array, layer = item
            rest = array.shape[1:]
            arrays.append(array)
            specs.append(
                pl.BlockSpec((None,) + rest, functools.partial(lambda l, n, i: (l,) + (0,) * n, layer, len(rest)))
            )
        else:
            arrays.append(item)
            specs.append(pl.BlockSpec(item.shape, functools.partial(lambda n, i: (0,) * n, item.ndim)))

    def kernel(*refs):
        results = body(*[r[...] for r in refs[: len(arrays)]])
        for ref, result in zip(refs[len(arrays) :], results):
            ref[...] = result

    shapes = [jax.ShapeDtypeStruct(s, t) for s, t in outs]
    return pl.pallas_call(
        kernel,
        grid=(1,),
        out_shape=shapes,
        in_specs=specs,
        out_specs=[pl.BlockSpec(s, functools.partial(lambda n, i: (0,) * n, len(s))) for s, _ in outs],
        compiler_params=pltpu.CompilerParams(vmem_limit_bytes=48 * 1024 * 1024),
        name=body.__name__,
    )(*arrays)


def wide(v):
    return v.astype(F32)


def dot(a, b):
    return lax.dot_general(a, b, (((1,), (0,)), ((), ())), preferred_element_type=F32)


def dot_nt(a, b):
    return lax.dot_general(a, b, (((1,), (1,)), ((), ())), preferred_element_type=F32)


def dot_tn(a, b):
    return lax.dot_general(a, b, (((0,), (0,)), ((), ())), preferred_element_type=F32)


def turn(v, by):
    size = v.shape[1]
    if KERNELS:
        return pltpu.roll(v, (-by) % size, 1)
    return jnp.roll(v, -by, axis=1)


def norm_parts(rows):
    centred = rows - jnp.mean(rows, axis=-1, keepdims=True)
    rstd = lax.rsqrt(jnp.mean(centred * centred, axis=-1, keepdims=True) + 1e-05)
    return centred * rstd, rstd


def norm_rows(rows, gain, shift):
    return norm_parts(rows)[0] * wide(gain) + wide(shift)


def norm_back(rows, gain, grad):
    hat, rstd = norm_parts(rows)
    d_hat = grad * wide(gain)
    d_rows = rstd * (
        d_hat
        - jnp.mean(d_hat, axis=-1, keepdims=True)
        - hat * jnp.mean(d_hat * hat, axis=-1, keepdims=True)
    )
    return d_rows, jnp.sum(grad * hat, axis=0, keepdims=True), jnp.sum(grad, axis=0, keepdims=True)


def paired(v):
    rest = jnp.log1p(jnp.exp(-jnp.abs(v)))
    return jnp.concatenate([jnp.maximum(v, 0.0) + rest, jnp.maximum(-v, 0.0) + rest], axis=1)


def features(v):
    c = paired(v)
    return jnp.concatenate([c * turn(c, 1), c * turn(c, 2), c * turn(c, 3)], axis=1)


def features_back(v, grad):
    c = paired(v)
    size = c.shape[1]
    d_c = jnp.zeros_like(c)
    for k in (1, 2, 3):
        part = grad[:, (k - 1) * size : k * size]
        d_c = d_c + part * turn(c, k) + turn(part * c, -k)
    half = v.shape[1]
    up = 1.0 / (1.0 + jnp.exp(-v))
    return d_c[:, :half] * up - d_c[:, half:] * (1.0 - up)


def write_keys(x, gains, shifts, assoc):
    normed = norm_rows(x, gains[0:1], shifts[0:1]).astype(BF)
    return (normed,)


def read_features(normed, assoc):
    keys = dot_nt(normed, assoc[: assoc.shape[0] // 2]).astype(BF)
    return (keys, features(wide(keys)).astype(BF))


def write_scores(tails, assoc, feat_q, mask):
    tail_keys = dot_nt(tails, assoc[assoc.shape[0] // 2 :])
    feat_k = features(tail_keys).astype(BF)
    scores = dot_nt(feat_q, feat_k) * mask
    denom = jnp.sum(scores, axis=1, keepdims=True) + 1.0
    return (tail_keys, feat_k, scores.astype(BF), jnp.broadcast_to(denom, mask.shape))


def write_values(tails, w_write):
    return (dot(tails, w_write).astype(BF),)


def read_memory(x, scores, values, denom, gains, shifts):
    read = (dot(scores, values) / denom[:, 0:1]).astype(BF)
    mid = x + wide(read)
    return (mid, norm_rows(mid, gains[1:2], shifts[1:2]).astype(BF))


def head_parts(packed, head):
    at = 3 * HD * head
    return packed[:, at : at + HD], packed[:, at + HD : at + 2 * HD], packed[:, at + 2 * HD : at + 3 * HD]


def head_probs(queries, keys, seen):
    scores = jnp.where(seen, dot_nt(queries, keys) * 0.125, -1e30)
    weights = jnp.exp(scores - jnp.max(scores, axis=1, keepdims=True))
    return weights / jnp.sum(weights, axis=1, keepdims=True)


def seen_rows(pos_rows, pos_cols):
    return pos_rows[:, 0:1] >= pos_cols[0:1, :]


def attention(own, other, w0, w1, bias0, bias1, o0, o1, pos_rows, pos_cols):
    rows = jnp.concatenate([own, other], axis=0)
    seen = seen_rows(pos_rows, pos_cols)
    half = own.shape[0]
    total, saved = 0.0, []
    for w, bias, o in ((w0, bias0, o0), (w1, bias1, o1)):
        packed = (dot(rows, w) + bias).astype(BF)
        mixed = []
        for head in range(packed.shape[1] // (3 * HD)):
            queries, keys, values = head_parts(packed, head)
            probs = head_probs(queries, keys, seen)
            mixed.append(dot(probs.astype(BF), values).astype(BF))
        mixed = jnp.concatenate(mixed, axis=1)
        total = total + dot(mixed, o)
        saved += [packed, mixed]
    return (total[:half], total[half:].astype(BF), saved[0], saved[2], saved[1], saved[3])


def after_attention(mid, part, arrived, bias, gains, shifts):
    after = mid + part + wide(arrived) + wide(bias[0:1])
    return (after, norm_rows(after, gains[2:3], shifts[2:3]).astype(BF))


def gelu_both(v):
    inner = 0.7978845608028654 * (v + 0.044715 * v * v * v)
    t = jnp.tanh(inner)
    slope = 0.5 * (1.0 + t) + 0.5 * v * (1.0 - t * t) * 0.7978845608028654 * (1.0 + 3 * 0.044715 * v * v)
    return 0.5 * v * (1.0 + t), slope


def feed_forward(own, other, w0, w1, bias0, bias1, p0, p1):
    rows = jnp.concatenate([own, other], axis=0)
    half = own.shape[0]
    total, hiddens, slopes = 0.0, [], []
    for w, bias, p in ((w0, bias0, p0), (w1, bias1, p1)):
        hidden, slope = gelu_both(dot(rows, w) + bias)
        hidden = hidden.astype(BF)
        total = total + dot(hidden, p)
        hiddens.append(hidden)
        slopes.append(slope.astype(BF))
    return (total[:half], total[half:].astype(BF), *hiddens, *slopes)


def after_feed(after, part, arrived, bias, next_gains, next_shifts):
    x = after + part + wide(arrived) + wide(bias[1:2])
    return (x, norm_rows(x, next_gains[0:1], next_shifts[0:1]).astype(BF))


def feed_back(own, other, w0, w1, p0, p1, slope0, slope1):
    grads = jnp.concatenate([own, other], axis=0)
    half = own.shape[0]
    total, saved = 0.0, []
    for w, p, slope in ((w0, p0, slope0), (w1, p1, slope1)):
        d_pre = (dot_nt(grads, p) * wide(slope)).astype(BF)
        total = total + dot_nt(d_pre, w)
        saved.append(d_pre)
    return (total[:half], total[half:].astype(BF), *saved)


def after_feed_back(grad, part, arrived, after, gains):
    d_rows, d_gain, d_shift = norm_back(after, gains[2:3], part + wide(arrived))
    d_after = grad + d_rows
    d_bias = jnp.sum(grad, axis=0, keepdims=True)
    return (d_after, d_after.astype(BF), d_gain, d_shift, d_bias)


def attention_back(own, other, w0, w1, o0, o1, packed0, packed1, pos_rows, pos_cols):
    grads = jnp.concatenate([own, other], axis=0)
    seen = seen_rows(pos_rows, pos_cols)
    half = own.shape[0]
    total, saved = 0.0, []
    for w, o, packed in ((w0, o0, packed0), (w1, o1, packed1)):
        d_mixed = dot_nt(grads, o).astype(BF)
        pieces = []
        for head in range(packed.shape[1] // (3 * HD)):
            queries, keys, values = head_parts(packed, head)
            dm = d_mixed[:, HD * head : HD * (head + 1)]
            probs = head_probs(queries, keys, seen)
            d_probs = dot_nt(dm, values)
            d_values = dot_tn(probs.astype(BF), dm)
            d_scores = (probs * (d_probs - jnp.sum(d_probs * probs, axis=1, keepdims=True))).astype(BF)
            pieces += [dot(d_scores, keys) * 0.125, dot_tn(d_scores, queries) * 0.125, d_values]
        d_packed = jnp.concatenate(pieces, axis=1).astype(BF)
        total = total + dot_nt(d_packed, w)
        saved.append(d_packed)
    return (total[:half], total[half:].astype(BF), *saved)


def after_attention_back(d_after, part, arrived, mid, gains, scores, values, denom, mask, feat_q, tail_keys):
    d_rows, d_gain, d_shift = norm_back(mid, gains[1:2], part + wide(arrived))
    d_mid = d_after + d_rows
    d_bias = jnp.sum(d_after, axis=0, keepdims=True)
    scale = 1.0 / denom[:, 0:1]
    d_numer = (d_mid * scale).astype(BF)
    d_denom = -jnp.sum(d_mid * dot(scores, values), axis=1, keepdims=True) * scale * scale
    d_scores = ((dot_nt(d_numer, values) + d_denom) * mask).astype(BF)
    d_keys = features_back(tail_keys, dot_tn(d_scores, feat_q))
    d_values = dot_tn(scores, d_numer)
    return (d_mid, d_scores, d_keys, d_values, d_gain, d_shift, d_bias)


def read_back(d_scores, feat_k, keys, assoc):
    d_keys = features_back(wide(keys), dot(d_scores, feat_k)).astype(BF)
    return (d_keys, dot(d_keys, assoc[: assoc.shape[0] // 2]))


def tail_back(d_keys, d_values, assoc, w_write):
    d_tail = dot(d_keys.astype(BF), assoc[assoc.shape[0] // 2 :]) + dot_nt(d_values.astype(BF), w_write)
    return (d_tail, d_values.astype(BF))


def layer_end_back(d_mid, d_norm, d_tail, x, gains):
    rows = d_norm.shape[0]
    d_norm = jnp.concatenate([d_norm[: rows - NMEM], d_norm[rows - NMEM :] + d_tail], axis=0)
    d_rows, d_gain, d_shift = norm_back(x, gains[0:1], d_norm)
    d_x = d_mid + d_rows
    return (d_x, d_x.astype(BF), d_gain, d_shift)


def two_products(a0, a1, a2, b0, b1):
    own = dot_tn(a0, b0) + dot_tn(jnp.concatenate([a1, a2], axis=0), b1)
    return (own.astype(BF),)


def toward(x, axis, bit):
    size = lax.axis_size(axis)
    return lax.ppermute(x, axis, [(i, i ^ bit) for i in range(size)])


def core_swap(x):
    return toward(x, "tp", 1)


def half_swap(x):
    return toward(x, "tp", 2)


def gather_segments(x):
    size = lax.axis_size("seg")
    me = lax.axis_index("seg")
    odd = (me & 1) == 1
    near = toward(x, "seg", 1)
    pair = jnp.where(odd, jnp.concatenate([near, x]), jnp.concatenate([x, near]))
    if size > 8:
        whole = lax.all_gather(x, "seg", axis=0, tiled=True)
        return whole
    whole = jnp.zeros((size // 2,) + pair.shape, x.dtype)
    for far in range(0, size, 2):
        other = toward(pair, "seg", far) if far else pair
        whole = lax.dynamic_update_slice(whole, other[None], ((me ^ far) // 2, 0, 0))
    return whole.reshape(-1, x.shape[1])


def scatter_segments(x):
    size = lax.axis_size("seg")
    blocks = lax.all_to_all(x.reshape(size, -1, x.shape[1]), "seg", 0, 0, tiled=True)
    return jnp.sum(wide(blocks), axis=0)


def sum_over_segments(x):
    size = lax.axis_size("seg")
    me = lax.axis_index("seg")
    bit = 1
    while bit < size:
        count = x.shape[0]
        halves = x.reshape((count // 2, 2) + x.shape[1:])
        mine = (me & bit) // bit
        keep = lax.dynamic_index_in_dim(halves, mine, 1, keepdims=False)
        send = lax.dynamic_index_in_dim(halves, 1 - mine, 1, keepdims=False)
        total = wide(keep) + wide(toward(send, "seg", bit))
        bit *= 2
        x = total if bit >= size else total.astype(BF)
    return x[0]


def sum_over_all(x):
    for bit in (1, 2):
        x = x + toward(x, "tp", bit)
    bit = 1
    while bit < lax.axis_size("seg"):
        x = x + toward(x, "seg", bit)
        bit *= 2
    return x


def fetch_other(w):
    odd = lax.axis_index("seg") & 1
    rows = w.shape[0] // 2
    part = half_swap(lax.dynamic_slice_in_dim(w, odd * rows, rows, axis=0))
    rest = toward(part, "seg", 1)
    first = odd == 0
    return jnp.where(
        first, jnp.concatenate([part, rest]), jnp.concatenate([rest, part])
    )


def local(
    tokens,
    mem_tokens,
    segno,
    gains,
    shifts,
    assoc,
    w_write,
    w_qkv,
    b_query_value,
    w_out,
    out_bias,
    w_fc,
    b_fc,
    w_proj,
    cot_tokens,
    cot_memory,
):
    mem_rows = mem_tokens.shape[0]
    block_rows = mem_rows + tokens.shape[2]
    own_rows = 2 * block_rows
    all_rows = 2 * own_rows
    segs = lax.axis_size("seg")
    me = lax.axis_index("seg")
    tp = lax.axis_index("tp")
    half, core = tp // 2, tp % 2
    slots = segs * NMEM
    key_dim = assoc.shape[1] // 2
    heads = w_qkv.shape[2] // (3 * HD)
    units = w_fc.shape[2]
    phi = 6 * key_dim

    def pick(pair, which):
        return lax.dynamic_index_in_dim(pair, which, 0, keepdims=False)

    def in_order(own, other):
        return jnp.where(half == 0, jnp.concatenate([own, other]), jnp.concatenate([other, own]))

    both = jnp.concatenate([jnp.broadcast_to(mem_tokens, (2,) + mem_tokens.shape), tokens[:, 0]], axis=1)
    x = wide(in_order(pick(both, half), half_swap(pick(both, 1 - half))))
    cots = jnp.concatenate([cot_memory[:, 0], cot_tokens[:, 0]], axis=1)

    bias_rows = jnp.concatenate([b_query_value, b_fc], axis=1)
    other_bias = half_swap(bias_rows)
    weights = []
    for l in range(LAYERS):
        other_write = fetch_other(w_write[l])
        mine = jnp.stack([w_write[l], other_write])
        mine = jnp.where(half == 0, mine, mine[::-1])
        theirs = core_swap(mine)
        left, right = jnp.where(core == 0, mine, theirs), jnp.where(core == 0, theirs, mine)
        full_write = jnp.concatenate([left[0], right[0], left[1], right[1]], axis=1)

        def spread_bias(row):
            parts = wide(row[: 2 * heads * HD]).reshape(heads, 2, HD)
            filled = jnp.stack([parts[:, 0], jnp.zeros_like(parts[:, 0]), parts[:, 1]], axis=1)
            return filled.reshape(1, -1), wide(row[2 * heads * HD :]).reshape(1, -1)

        qkv_bias, fc_bias = spread_bias(bias_rows[l])
        other_qkv_bias, other_fc_bias = spread_bias(other_bias[l])
        weights.append(
            dict(
                write=full_write,
                qkv=((w_qkv, l), fetch_other(w_qkv[l])),
                out=((w_out, l), fetch_other(w_out[l])),
                fc=((w_fc, l), fetch_other(w_fc[l])),
                proj=((w_proj, l), fetch_other(w_proj[l])),
                qkv_bias=(qkv_bias, other_qkv_bias),
                fc_bias=(fc_bias, other_fc_bias),
                gains=(gains, l),
                shifts=(shifts, l),
                assoc=(assoc, l),
                bias=(out_bias, l),
            )
        )

    def places(core_id):
        within = jnp.arange(block_rows)
        rows = []
        for block in (core_id, core_id + 2):
            rows.append(
                jnp.where(
                    within < mem_rows,
                    block * mem_rows + within,
                    4 * mem_rows + block * (block_rows - mem_rows) + within - mem_rows,
                )
            )
        return jnp.concatenate(rows)

    pos = jnp.concatenate([places(core), places(1 - core)]).astype(jnp.int32)
    pos_rows = jnp.broadcast_to(pos[:, None], (all_rows, 128))
    pos_cols = jnp.broadcast_to(pos[None, :], (8, all_rows))
    number = lax.dynamic_index_in_dim(segno[:, 0], half, 0, keepdims=False)
    segment_of = jnp.arange(slots) // NMEM
    mask = jnp.broadcast_to(
        ((segment_of < me) & (segment_of >= me - number)).astype(F32)[None, :], (own_rows, slots)
    )

    saved = []
    (normed,) = phase(
        write_keys, [((own_rows, D), BF)], x, weights[0]["gains"], weights[0]["shifts"], weights[0]["assoc"]
    )
    for l in range(LAYERS):
        w = weights[l]
        tail_own = normed[own_rows - NMEM :]
        tail = jnp.where(core == 1, tail_own, core_swap(tail_own))
        tails = gather_segments(tail)
        keys, feat_q = phase(
            read_features, [((own_rows, key_dim), BF), ((own_rows, phi), BF)], normed, w["assoc"]
        )
        tail_keys, feat_k, scores, denom = phase(
            write_scores,
            [((slots, key_dim), F32), ((slots, phi), BF), ((own_rows, slots), BF), ((own_rows, slots), F32)],
            tails,
            w["assoc"],
            feat_q,
            mask,
        )
        (values,) = phase(write_values, [((slots, D), BF)], tails, w["write"])
        mid, normed1 = phase(
            read_memory,
            [((own_rows, D), F32), ((own_rows, D), BF)],
            x,
            scores,
            values,
            denom,
            w["gains"],
            w["shifts"],
        )
        normed1_core = core_swap(normed1)
        part, sent, packed0, packed1, mixed0, mixed1 = phase(
            attention,
            [((own_rows, D), F32), ((own_rows, D), BF)]
            + [((all_rows, 3 * HD * heads), BF)] * 2
            + [((all_rows, HD * heads), BF)] * 2,
            normed1,
            normed1_core,
            *w["qkv"],
            *w["qkv_bias"],
            *w["out"],
            pos_rows,
            pos_cols,
        )
        after, normed2 = phase(
            after_attention,
            [((own_rows, D), F32), ((own_rows, D), BF)],
            mid,
            part,
            core_swap(sent),
            w["bias"],
            w["gains"],
            w["shifts"],
        )
        normed2_core = core_swap(normed2)
        part, sent, hidden0, hidden1, slope0, slope1 = phase(
            feed_forward,
            [((own_rows, D), F32), ((own_rows, D), BF)] + [((all_rows, units), BF)] * 4,
            normed2,
            normed2_core,
            *w["fc"],
            *w["fc_bias"],
            *w["proj"],
        )
        later = weights[min(l + 1, LAYERS - 1)]
        x_next, normed_next = phase(
            after_feed,
            [((own_rows, D), F32), ((own_rows, D), BF)],
            after,
            part,
            core_swap(sent),
            w["bias"],
            later["gains"],
            later["shifts"],
        )
        saved.append(
            dict(
                x=x, normed=normed, tails=tails, keys=keys, feat_q=feat_q, tail_keys=tail_keys, feat_k=feat_k,
                scores=scores, denom=denom, values=values, mid=mid, normed1=(normed1, normed1_core),
                packed=(packed0, packed1), mixed=(mixed0, mixed1), after=after,
                normed2=(normed2, normed2_core), hidden=(hidden0, hidden1), slope=(slope0, slope1),
            )
        )
        x, normed = x_next, normed_next

    def give_back(rows):
        blocks = rows.reshape(2, block_rows, -1)
        mine = pick(blocks, half)
        got = half_swap(pick(blocks, 1 - half))
        return jnp.where(half == 0, jnp.stack([mine, got]), jnp.stack([got, mine]))

    result = give_back(x.astype(BF))
    out_memory = result[:, :mem_rows][:, None]
    out_tokens = result[:, mem_rows:][:, None]

    grad_low = in_order(pick(cots, half), half_swap(pick(cots, 1 - half)))
    grad = wide(grad_low)
    vec = ((1, D), F32)
    layer_grads = [None] * LAYERS
    small = [None] * LAYERS

    def both_halves(own, core_rows):
        got = half_swap(own)
        return own, core_rows, got, core_swap(got)

    def wide_product(rows, own, other):
        first, second, third, fourth = rows
        arrived = half_swap(other)
        product = dot_tn(jnp.concatenate([first, second]), own) + dot_tn(jnp.concatenate([third, fourth]), arrived)
        sums = jnp.sum(wide(own), axis=0) + jnp.sum(wide(arrived), axis=0)
        return product.astype(BF), sums

    for l in reversed(range(LAYERS)):
        w, s = weights[l], saved[l]
        grad_core = core_swap(grad_low)
        part, sent, d_pre0, d_pre1 = phase(
            feed_back,
            [((own_rows, D), F32), ((own_rows, D), BF)] + [((all_rows, units), BF)] * 2,
            grad_low,
            grad_core,
            *w["fc"],
            *w["proj"],
            *s["slope"],
        )
        d_after, d_after_low, d_gain2, d_shift2, d_bias1 = phase(
            after_feed_back,
            [((own_rows, D), F32), ((own_rows, D), BF), vec, vec, vec],
            grad,
            part,
            core_swap(sent),
            s["after"],
            w["gains"],
        )
        d_after_core = core_swap(d_after_low)
        g_fc, g_bfc = wide_product(both_halves(*s["normed2"]), d_pre0, d_pre1)
        g_proj, _ = wide_product(both_halves(grad_low, grad_core), *s["hidden"])
        part, sent, d_packed0, d_packed1 = phase(
            attention_back,
            [((own_rows, D), F32), ((own_rows, D), BF)] + [((all_rows, 3 * HD * heads), BF)] * 2,
            d_after_low,
            d_after_core,
            *w["qkv"],
            *w["out"],
            *s["packed"],
            pos_rows,
            pos_cols,
        )
        d_mid, d_scores, d_keys, d_values, d_gain1, d_shift1, d_bias0 = phase(
            after_attention_back,
            [((own_rows, D), F32), ((own_rows, slots), BF), ((slots, key_dim), F32), ((slots, D), F32), vec, vec, vec],
            d_after,
            part,
            core_swap(sent),
            s["mid"],
            w["gains"],
            s["scores"],
            s["values"],
            s["denom"],
            mask,
            s["feat_q"],
            s["tail_keys"],
        )
        key_halves = jnp.stack([d_keys[:, : key_dim // 2], d_keys[:, key_dim // 2 :]])
        value_halves = jnp.stack([d_values[:, : D // 2], d_values[:, D // 2 :]])
        halves = jnp.concatenate([key_halves, value_halves], axis=2)
        written = pick(halves, core) + wide(core_swap(pick(halves, 1 - core).astype(BF)))
        written = scatter_segments(written.astype(BF))
        written_core = core_swap(written)
        left, right = jnp.where(core == 0, written, written_core), jnp.where(core == 0, written_core, written)
        cut = key_dim // 2
        d_tail, d_vals = phase(
            tail_back,
            [((NMEM, D), F32), ((NMEM, D), BF)],
            jnp.concatenate([left[:, :cut], right[:, :cut]], axis=1),
            jnp.concatenate([left[:, cut:], right[:, cut:]], axis=1),
            w["assoc"],
            w["write"],
        )
        d_tail = jnp.where(core == 1, d_tail, 0.0)
        d_read_keys, d_norm = phase(
            read_back, [((own_rows, key_dim), BF), ((own_rows, D), F32)], d_scores, s["feat_k"], s["keys"], w["assoc"]
        )
        d_x, d_x_low, d_gain0, d_shift0 = phase(
            layer_end_back,
            [((own_rows, D), F32), ((own_rows, D), BF), vec, vec],
            d_mid,
            d_norm,
            d_tail,
            s["x"],
            w["gains"],
        )
        g_qkv, sums = wide_product(both_halves(*s["normed1"]), d_packed0, d_packed1)
        g_out, _ = wide_product(both_halves(d_after_low, d_after_core), *s["mixed"])
        tail_own = s["normed"][own_rows - NMEM :]
        tail = jnp.where(core == 1, tail_own, core_swap(tail_own))
        columns = w_write.shape[2]
        blocks = jnp.moveaxis(d_vals.reshape(NMEM, 4, columns), 1, 0)
        other_vals = half_swap(pick(blocks, tp ^ 2))
        g_write = (dot_tn(tail, pick(blocks, tp)) + dot_tn(half_swap(tail), other_vals)).astype(BF)
        g_assoc = jnp.concatenate(
            [dot_tn(s["normed"], d_read_keys), dot_tn(s["tails"], d_keys.astype(BF))], axis=1
        ).astype(BF)
        g_assoc = g_assoc.reshape(segs, 2, 2, -1, 2 * key_dim)
        for which, bit, dim in ((core, 1, 2), (half, 2, 1)):
            keep = lax.dynamic_index_in_dim(g_assoc, which, dim, keepdims=False)
            send = lax.dynamic_index_in_dim(g_assoc, 1 - which, dim, keepdims=False)
            g_assoc = (wide(keep) + wide(toward(send, "tp", bit))).astype(BF)

        def owned(g):
            return sum_over_segments(g.reshape(segs, g.shape[0] // segs, g.shape[1]))

        bias_sums = sums.reshape(heads, 3, HD)
        g_qv = jnp.stack([bias_sums[:, 0], bias_sums[:, 2]], axis=1).reshape(-1)
        layer_grads[l] = dict(
            fc=owned(g_fc),
            proj=owned(g_proj).T,
            qkv=owned(g_qkv),
            out=owned(g_out).T,
            write=owned(g_write),
            assoc=sum_over_segments(g_assoc).T,
        )
        qv_full = lax.dynamic_update_slice(jnp.zeros((4 * g_qv.shape[0],), F32), g_qv, (tp * g_qv.shape[0],))
        bfc_full = lax.dynamic_update_slice(jnp.zeros((4 * units,), F32), g_bfc, (tp * units,))
        rows = [d_gain0, d_gain1, d_gain2, d_shift0, d_shift1, d_shift2, d_bias0, d_bias1]
        rows += [qv_full.reshape(-1, D), bfc_full.reshape(-1, D)]
        if l == 0:
            kept = d_x.reshape(2, block_rows, D)[:, :mem_rows]
            mem_full = lax.dynamic_update_slice(
                jnp.zeros((2, 2, mem_rows, D), F32), kept[:, None], (0, core, 0, 0)
            )
            rows.append(mem_full.reshape(-1, D))
        small[l] = sum_over_all(jnp.concatenate(rows))
        grad, grad_low = d_x, d_x_low

    result = give_back(grad)
    grad_tokens = result[:, mem_rows:][:, None]
    at = me * 4 + tp

    def own_columns(rows):
        return lax.dynamic_slice_in_dim(rows, at * (D // (4 * segs)), D // (4 * segs), axis=1)

    def own_entries(rows):
        flat = rows.reshape(1, -1)
        size = flat.shape[1] // (4 * segs)
        return lax.dynamic_slice_in_dim(flat, at * size, size, axis=1)[0]

    columns = [own_columns(r) for r in small]
    qv_rows = 2 * D // D
    stacked = {k: jnp.stack([layer_grads[l][k] for l in range(LAYERS)]) for k in layer_grads[0]}
    return (
        out_tokens,
        out_memory,
        grad_tokens,
        columns[0][14:],
        jnp.stack([c[0:3] for c in columns]),
        jnp.stack([c[3:6] for c in columns]),
        stacked["assoc"],
        stacked["write"],
        stacked["qkv"],
        jnp.stack([own_entries(r[8 : 8 + qv_rows]) for r in small]),
        stacked["out"],
        jnp.stack([c[6:8] for c in columns]),
        stacked["fc"],
        jnp.stack([own_entries(r[8 + qv_rows : 14]) for r in small]),
        stacked["proj"],
    )


def solution(mesh):
    return jax.shard_map(
        local,
        mesh=mesh,
        in_specs=(
            P(None, "seg", "tp", None),
            P("tp", None),
            P(None, "seg"),
            P(),
            P(),
            P(),
            P(None, None, "tp"),
            P(None, None, "tp"),
            P(None, "tp"),
            P(None, "tp", None),
            P(),
            P(None, None, "tp"),
            P(None, "tp"),
            P(None, "tp", None),
            P(None, "seg", "tp", None),
            P(None, "seg", "tp", None),
        ),
        out_specs=(
            P(None, "seg", "tp", None),
            P(None, "seg", "tp", None),
            P(None, "seg", "tp", None),
            P(None, ("seg", "tp")),
            P(None, None, ("seg", "tp")),
            P(None, None, ("seg", "tp")),
            P(None, None, ("seg", "tp")),
            P(None, "seg", "tp"),
            P(None, "seg", "tp"),
            P(None, ("seg", "tp")),
            P(None, "tp", "seg"),
            P(None, None, ("seg", "tp")),
            P(None, "seg", "tp"),
            P(None, ("seg", "tp")),
            P(None, "tp", "seg"),
        ),
        check_vma=False,
    )
```

time: 1790 us -> 625 us (0.35)
  waiting for transfers between devices: 1190 us -> 153 us
  blocking collectives: 146 us -> 0 us
  starting transfers between devices: 14 us -> 142 us
  matrix products: 131 us -> 32.1 us
  Pallas kernels: 0 us -> 55.4 us
  other arithmetic: 110 us -> 70.5 us
    reduce_scatter x16 -> x0, waiting for transfers between devices: 620 us -> none  [the longest x10 186 us: collect(): lax.psum_scatter(to_blocks(full, mem_rows, lax.axis_size('tp')).astype(jn...]
    unnamed x30 -> x0, waiting for transfers between devices: 525 us -> none
    ppermute x0 -> x135, waiting for transfers between devices: none -> 153 us  [toward(): return lax.ppermute(x, axis, [(i, i ^ bit) for i in range(size)])]
    ppermute x0 -> x135, starting transfers between devices: none -> 133 us  [toward(): return lax.ppermute(x, axis, [(i, i ^ bit) for i in range(size)])]
    all_gather x10 -> x0, blocking collectives: 129 us -> none  [the longest x8 67.2 us: spread(): lax.all_gather(own, 'tp', axis=1, tiled=True)]
    dot_general x70 -> x24, matrix products: 126 us -> 32.1 us  [dot_tn(): lax.dot_general(a, b, (((0,), (0,)), ((), ())), preferred_element_type=F32)]
    pallas_call x0 -> x31, Pallas kernels: none -> 55.4 us  [phase(): pl.pallas_call(kernel, grid=(1,), out_shape=shapes, in_specs=specs, out_s...]
    all_gather x4 -> x0, waiting for transfers between devices: 37.6 us -> none  [the longest x2 37.6 us: spread(): lax.all_gather(own, 'tp', axis=1, tiled=True)]
  transfers between devices with their start and end apart: 28 -> 137, of which waited for: 24 -> 51; matrix products, arithmetic and copies ran while one was open for 9% -> 35% of each run, Pallas kernels for 0% -> 9%
where the time goes in v1:
time: 625 us; the launch traced here: 618 us
  local copies, waits for them, and re-layouts  160 us (26%)
  waiting for transfers between devices  153 us (24%)
  starting transfers between devices  142 us (23%)
  other arithmetic  70.5 us (11%)
  Pallas kernels  55.4 us (9%)
  matrix products  32.1 us (5%)
    ppermute x135, waiting for transfers between devices, toward(): return lax.ppermute(x, axis, [(i, i ^ bit) for i in range(size)])  153 us
    ppermute x135, starting transfers between devices, toward(): return lax.ppermute(x, axis, [(i, i ^ bit) for i in range(size)])  133 us
    unnamed x569, local copies, waits for them, and re-layouts  64.8 us
    pallas_call x31, Pallas kernels, phase(): pl.pallas_call(kernel, grid=(1,), out_shape=shapes, in_specs=specs, out_s...  55.4 us
    dot_general x24, matrix products, dot_tn(): lax.dot_general(a, b, (((0,), (0,)), ((), ())), preferred_element_type=F32)  32.1 us
    squeeze x32, local copies, waits for them, and re-layouts, sum_over_segments(): send = lax.dynamic_index_in_dim(halves, 1 - mine, 1, keepdims=False)  14.4 us
    select_n x10, other arithmetic, fetch_other(): jnp.where(first, jnp.concatenate([part, rest]), jnp.concatenate([rest, pa...  13.1 us
  transfers between devices with their start and end apart: 137, of which 51 were waited for; matrix products, arithmetic and copies ran while one was open for 35% of the time, Pallas kernels for 9%

profile of v1, /device:TPU:0, one launch (start us, length us, event | category | flops | bytes accessed | tf_op | source)
XLA Modules:
  0.0 617.7 jit_solution(12485494156168420831)
XLA Ops:
  3.1 3.0 collective-permute-start
  11.9 2.8 fusion.139
  19.9 2.9 fusion.140
  32.6 2.5 copy.140.refs_2_
  60.4 2.6 collective-permute-start.4
  65.8 3.0 collective-permute-done.27
  90.3 5.0 collective-permute-done.10
  113.3 4.2 attention.2
  138.1 4.6 feed_forward.2
  148.8 2.5 collective-permute-done.23
  156.2 3.0 collective-permute-start.25
  161.4 4.9 collective-permute-start.26
  177.9 3.6 attention.3
  184.5 3.0 collective-permute-done.38
  188.0 7.2 %collective-permute-done.40 = bf16[384,768]{1,0:T(8,128)(2,1)S(1)} collective-permute-done((bf16[384,768]{1,0:T(8,128)(2,1)S(1)}, bf16[384,768]{1,0:T(8,128)(2,1)S(1)}, u32[]{:S(2)}, u32[]{:S(2)}) %collective-permute-start.40) | collective-permute-done | bytes 589856 | tf_op jit(solution)/shard_map/ppermute | solution.py:291
  195.8 4.9 feed_forward.3
  212.7 3.8 feed_back.2
  224.0 6.6 %collective-permute-done.42 = bf16[64,768]{1,0:T(8,128)(2,1)S(1)} collective-permute-done((bf16[64,768]{1,0:T(8,128)(2,1)S(1)}, bf16[64,768]{1,0:T(8,128)(2,1)S(1)}, u32[]{:S(2)}, u32[]{:S(2)}) %collective-permute-start.42) | collective-permute-done | bytes 98336 | tf_op jit(solution)/shard_map/ppermute | solution.py:291
  236.6 11.6 %collective-permute-done.131 = bf16[256,768]{1,0:T(8,128)(2,1)S(1)} collective-permute-done((bf16[256,768]{1,0:T(8,128)(2,1)S(1)}, bf16[256,768]{1,0:T(8,128)(2,1)S(1)}, u32[]{:S(2)}, u32[]{:S(2)}) %collective-permute-start.131) | collective-permute-done | bytes 393248 | tf_op jit(solution)/shard_map/ppermute | solution.py:291
  250.1 2.7 add_convert_fusion
  257.4 6.1 attention_back.2
  280.7 3.0 constant_dynamic-slice_fusion.10
  300.8 10.1 %collective-permute-done.110 = bf16[4,96,192]{2,1,0:T(8,128)(2,1)} collective-permute-done((bf16[4,96,192]{2,1,0:T(8,128)(2,1)}, bf16[4,96,192]{2,1,0:T(8,128)(2,1)}, u32[]{:S(2)}, u32[]{:S(2)}) %collective-permute-start.110) | collective-permute-done | bytes 147488 | tf_op jit(solution)/shard_map/ppermute | solution.py:291
  313.9 2.7 collective-permute-done.111
  318.7 4.6 all-to-all-start
  329.2 10.9 %collective-permute-done.132 = bf16[4,96,768]{2,1,0:T(8,128)(2,1)S(1)} collective-permute-done((bf16[4,96,768]{2,1,0:T(8,128)(2,1)}, bf16[4,96,768]{2,1,0:T(8,128)(2,1)S(1)}, u32[]{:S(2)}, u32[]{:S(2)}) %collective-permute-start.132) | collective-permute-done | bytes 589856 | tf_op jit(solution)/shard_map/ppermute | solution.py:291
  356.5 2.9 constant_dynamic-slice_fusion.20
  370.1 5.1 collective-permute-done.88
  376.6 2.6 collective-permute-done.69
  383.0 3.4 feed_back.3
  386.7 3.2 collective-permute-start.89
  393.1 2.5 collective-permute-start.133
  397.4 3.4 collective-permute-done.133
  403.1 2.7 collective-permute-done.90
  408.5 4.6 collective-permute-done.99
  415.3 5.4 collective-permute-done.122
  423.7 3.6 collective-permute-done.134
  434.5 3.4 collective-permute-done.77
  438.2 7.7 %collective-permute-done.100 = bf16[1,96,576]{2,1,0:T(8,128)(2,1)S(1)} collective-permute-done((bf16[1,96,576]{2,1,0:T(8,128)(2,1)S(1)}, bf16[1,96,576]{2,1,0:T(8,128)(2,1)S(1)}, u32[]{:S(2)}, u32[]{:S(2)}) %collective-permute-start.100) | collective-permute-done | bytes 110624 | tf_op jit(solution)/shard_map/ppermute | solution.py:291
  449.2 2.5 collective-permute-done.78
  456.7 5.8 attention_back.3
  521.4 4.2 all-to-all-start.1
  577.8 3.0 collective-permute-done.84
  584.0 5.2 collective-permute-done.85
  590.2 3.1 collective-permute-start.95
  593.3 2.9 collective-permute-done.62
  600.7 3.2 collective-permute-start.73
  607.3 4.3 collective-permute-done.74
  (1130 shorter events, 405.8 us)
Async XLA Ops:
  3.1 38.5 %collective-permute-start = (bf16[64,768]{1,0:T(8,128)(2,1)}, bf16[64,768]{1,0:T(8,128)(2,1)}, u32[]{:S(2)}, u32[]{:S(2)}) collective-permute-start(bf16[64,768]{1,0:T(8,128)(2,1)} %get-tuple-element.309), channel_id=1, source_target_pairs={{0,2},{1,3},{2,0},{3,1},{4,6},{5,7},{6,4},{7,5},{8,10},{9,11},{10,... | collective-permute-start | bytes 294920 | tf_op jit(solution)/shard_map/ppermute | solution.py:291
  7.8 55.2 %collective-permute-start.6 = (bf16[384,192]{1,0:T(8,128)(2,1)}, bf16[384,192]{1,0:T(8,128)(2,1)}, u32[]{:S(2)}, u32[]{:S(2)}) collective-permute-start(bf16[384,192]{1,0:T(8,128)(2,1)} %dynamic-slice_bitcast_fusion.20), channel_id=1, source_target_pairs={{0,2},{1,3},{2,0},{3,1},{4,6},{5,7},{6,4},{7,5},{8,10},{9,11},{10,... | collective-permute-start | bytes 442376 | tf_op jit(solution)/shard_map/ppermute | solution.py:291
  8.4 31.9 %collective-permute-start.12 = (bf16[2,1152]{1,0:T(2,128)(2,1)}, bf16[2,1152]{1,0:T(2,128)(2,1)S(1)}, u32[]{:S(2)}, u32[]{:S(2)}) collective-permute-start(bf16[2,1152]{1,0:T(2,128)(2,1)} %pad_maximum_fusion.20), channel_id=1, source_target_pairs={{0,2},{1,3},{2,0},{3,1},{4,6},{5,7},{6,4},{7,5},{8,10},{9,11},{10,... | collective-permute-start | bytes 13832 | tf_op jit(solution)/shard_map/ppermute | solution.py:291
  11.8 69.1 %collective-permute-start.13 = (bf16[96,768]{1,0:T(8,128)(2,1)}, bf16[96,768]{1,0:T(8,128)(2,1)}, u32[]{:S(2)}, u32[]{:S(2)}) collective-permute-start(bf16[96,768]{1,0:T(8,128)(2,1)} %dynamic-slice_bitcast_fusion.24), channel_id=1, source_target_pairs={{0,2},{1,3},{2,0},{3,1},{4,6},{5,7},{6,4},{7,5},{8,10},{9,11},{10,... | collective-permute-start | bytes 442376 | tf_op jit(solution)/shard_map/ppermute | solution.py:291
  15.6 79.7 %collective-permute-start.17 = (bf16[384,768]{1,0:T(8,128)(2,1)}, bf16[384,768]{1,0:T(8,128)(2,1)}, u32[]{:S(2)}, u32[]{:S(2)}) collective-permute-start(bf16[384,768]{1,0:T(8,128)(2,1)} %dynamic-slice_bitcast_fusion.7), channel_id=1, source_target_pairs={{0,2},{1,3},{2,0},{3,1},{4,6},{5,7},{6,4},{7,5},{8,10},{9,11},{10,... | collective-permute-start | bytes 1769480 | tf_op jit(solution)/shard_map/ppermute | solution.py:291
  40.3 56.7 %collective-permute-start.19 = (bf16[384,768]{1,0:T(8,128)(2,1)}, bf16[384,768]{1,0:T(8,128)(2,1)}, u32[]{:S(2)}, u32[]{:S(2)}) collective-permute-start(bf16[384,768]{1,0:T(8,128)(2,1)} %dynamic-slice_bitcast_fusion.6), channel_id=1, source_target_pairs={{0,2},{1,3},{2,0},{3,1},{4,6},{5,7},{6,4},{7,5},{8,10},{9,11},{10,... | collective-permute-start | bytes 1769480 | tf_op jit(solution)/shard_map/ppermute | solution.py:291
  77.3 20.0 %collective-permute-start.8 = (bf16[2,768,192]{1,2,0:T(8,128)(2,1)}, bf16[2,768,192]{1,2,0:T(8,128)(2,1)}, u32[]{:S(2)}, u32[]{:S(2)}) collective-permute-start(bf16[2,768,192]{1,2,0:T(8,128)(2,1)} %copy.134), channel_id=1, source_target_pairs={{0,1},{1,0},{2,3},{3,2},{4,5},{5,4},{6,7},{7,6},{8,9},{9,8},{10,11... | collective-permute-start | bytes 1769480 | tf_op jit(solution)/shard_map/ppermute | solution.py:291
  83.0 24.1 %collective-permute-start.14 = (bf16[96,768]{1,0:T(8,128)(2,1)}, bf16[96,768]{1,0:T(8,128)(2,1)}, u32[]{:S(2)}, u32[]{:S(2)}) collective-permute-start(bf16[96,768]{1,0:T(8,128)(2,1)} %collective-permute-done.13), channel_id=1, source_target_pairs={{0,4},{4,0},{8,12},{12,8},{16,20},{20,16},{24,28},{28,24},{1,5},{5... | collective-permute-start | bytes 442376 | tf_op jit(solution)/shard_map/ppermute | solution.py:291
  95.2 26.3 %collective-permute-start.29 = (bf16[2,768,192]{1,2,0:T(8,128)(2,1)}, bf16[2,768,192]{1,2,0:T(8,128)(2,1)}, u32[]{:S(2)}, u32[]{:S(2)}) collective-permute-start(bf16[2,768,192]{1,2,0:T(8,128)(2,1)} %copy.146), channel_id=1, source_target_pairs={{0,1},{1,0},{2,3},{3,2},{4,5},{5,4},{6,7},{7,6},{8,9},{9,8},{10,11... | collective-permute-start | bytes 1769480 | tf_op jit(solution)/shard_map/ppermute | solution.py:291
  97.0 32.8 %collective-permute-start.18 = (bf16[384,768]{1,0:T(8,128)(2,1)}, bf16[384,768]{1,0:T(8,128)(2,1)}, u32[]{:S(2)}, u32[]{:S(2)}) collective-permute-start(bf16[384,768]{1,0:T(8,128)(2,1)} %collective-permute-done.17), channel_id=1, source_target_pairs={{0,4},{4,0},{8,12},{12,8},{16,20},{20,16},{24,28},{28,24},{1,5},{5... | collective-permute-start | bytes 1769480 | tf_op jit(solution)/shard_map/ppermute | solution.py:291
  97.3 37.2 %collective-permute-start.20 = (bf16[384,768]{1,0:T(8,128)(2,1)}, bf16[384,768]{1,0:T(8,128)(2,1)}, u32[]{:S(2)}, u32[]{:S(2)}) collective-permute-start(bf16[384,768]{1,0:T(8,128)(2,1)} %collective-permute-done.19), channel_id=1, source_target_pairs={{0,4},{4,0},{8,12},{12,8},{16,20},{20,16},{24,28},{28,24},{1,5},{5... | collective-permute-start | bytes 1769480 | tf_op jit(solution)/shard_map/ppermute | solution.py:291
  109.6 22.4 %collective-permute-start.31 = (bf16[384,576]{1,0:T(8,128)(2,1)}, bf16[384,576]{1,0:T(8,128)(2,1)}, u32[]{:S(2)}, u32[]{:S(2)}) collective-permute-start(bf16[384,576]{1,0:T(8,128)(2,1)} %bitcast.34), channel_id=1, source_target_pairs={{0,2},{1,3},{2,0},{3,1},{4,6},{5,7},{6,4},{7,5},{8,10},{9,11},{10,... | collective-permute-start | bytes 1327112 | tf_op jit(solution)/shard_map/ppermute | solution.py:291
  121.6 44.6 %collective-permute-start.33 = (bf16[96,768]{1,0:T(8,128)(2,1)}, bf16[96,768]{1,0:T(8,128)(2,1)}, u32[]{:S(2)}, u32[]{:S(2)}) collective-permute-start(bf16[96,768]{1,0:T(8,128)(2,1)} %dynamic-slice_bitcast_fusion.23), channel_id=1, source_target_pairs={{0,2},{1,3},{2,0},{3,1},{4,6},{5,7},{6,4},{7,5},{8,10},{9,11},{10,... | collective-permute-start | bytes 442376 | tf_op jit(solution)/shard_map/ppermute | solution.py:291
  124.8 43.1 %collective-permute-start.37 = (bf16[384,768]{1,0:T(8,128)(2,1)}, bf16[384,768]{1,0:T(8,128)(2,1)S(1)}, u32[]{:S(2)}, u32[]{:S(2)}) collective-permute-start(bf16[384,768]{1,0:T(8,128)(2,1)} %dynamic-slice_bitcast_fusion.5), channel_id=1, source_target_pairs={{0,2},{1,3},{2,0},{3,1},{4,6},{5,7},{6,4},{7,5},{8,10},{9,11},{10,... | collective-permute-start | bytes 1769480 | tf_op jit(solution)/shard_map/ppermute | solution.py:291
  132.0 36.4 %collective-permute-start.39 = (bf16[384,768]{1,0:T(8,128)(2,1)S(1)}, bf16[384,768]{1,0:T(8,128)(2,1)S(1)}, u32[]{:S(2)}, u32[]{:S(2)}) collective-permute-start(bf16[384,768]{1,0:T(8,128)(2,1)S(1)} %copy-done.227), channel_id=1, source_target_pairs={{0,2},{1,3},{2,0},{3,1},{4,6},{5,7},{6,4},{7,5},{8,10},{9,11},{10,... | collective-permute-start | bytes 1769480 | tf_op jit(solution)/shard_map/ppermute | solution.py:291
  134.5 41.7 %collective-permute-start.32 = (bf16[384,576]{1,0:T(8,128)(2,1)}, bf16[384,576]{1,0:T(8,128)(2,1)S(1)}, u32[]{:S(2)}, u32[]{:S(2)}) collective-permute-start(bf16[384,576]{1,0:T(8,128)(2,1)} %collective-permute-done.31), channel_id=1, source_target_pairs={{0,4},{4,0},{8,12},{12,8},{16,20},{20,16},{24,28},{28,24},{1,5},{5... | collective-permute-start | bytes 1327112 | tf_op jit(solution)/shard_map/ppermute | solution.py:291
  168.4 19.1 %collective-permute-start.38 = (bf16[384,768]{1,0:T(8,128)(2,1)S(1)}, bf16[384,768]{1,0:T(8,128)(2,1)S(1)}, u32[]{:S(2)}, u32[]{:S(2)}) collective-permute-start(bf16[384,768]{1,0:T(8,128)(2,1)S(1)} %collective-permute-done.37), channel_id=1, source_target_pairs={{0,4},{4,0},{8,12},{12,8},{16,20},{20,16},{24,28},{28,24},{1,5},{5... | collective-permute-start | bytes 1769480 | tf_op jit(solution)/shard_map/ppermute | solution.py:291
  169.9 25.3 %collective-permute-start.40 = (bf16[384,768]{1,0:T(8,128)(2,1)S(1)}, bf16[384,768]{1,0:T(8,128)(2,1)S(1)}, u32[]{:S(2)}, u32[]{:S(2)}) collective-permute-start(bf16[384,768]{1,0:T(8,128)(2,1)S(1)} %collective-permute-done.39), channel_id=1, source_target_pairs={{0,4},{4,0},{8,12},{12,8},{16,20},{20,16},{24,28},{28,24},{1,5},{5... | collective-permute-start | bytes 1769480 | tf_op jit(solution)/shard_map/ppermute | solution.py:291
  182.9 25.2 %collective-permute-start.44 = (bf16[128,768]{1,0:T(8,128)(2,1)}, bf16[128,768]{1,0:T(8,128)(2,1)}, u32[]{:S(2)}, u32[]{:S(2)}) collective-permute-start(bf16[128,768]{1,0:T(8,128)(2,1)} %get-tuple-element.269.refs_0_), channel_id=1, source_target_pairs={{0,1},{1,0},{2,3},{3,2},{4,5},{5,4},{6,7},{7,6},{8,9},{9,8},{10,11... | collective-permute-start | bytes 589832 | tf_op jit(solution)/shard_map/ppermute | solution.py:291
  220.8 333.6 %collective-permute-start.81 = (bf16[16,768]{1,0:T(8,128)(2,1)}, bf16[16,768]{1,0:T(8,128)(2,1)}, u32[]{:S(2)}, u32[]{:S(2)}) collective-permute-start(bf16[16,768]{1,0:T(8,128)(2,1)} %broadcast_select_fusion.7), channel_id=1, source_target_pairs={{0,2},{1,3},{2,0},{3,1},{4,6},{5,7},{6,4},{7,5},{8,10},{9,11},{10,... | collective-permute-start | bytes 73736 | tf_op jit(solution)/shard_map/ppermute | solution.py:291
  222.4 225.2 %collective-permute-start.91 = (bf16[128,768]{1,0:T(8,128)(2,1)}, bf16[128,768]{1,0:T(8,128)(2,1)}, u32[]{:S(2)}, u32[]{:S(2)}) collective-permute-start(bf16[128,768]{1,0:T(8,128)(2,1)} %get-tuple-element.121.refs_0_), channel_id=1, source_target_pairs={{0,2},{1,3},{2,0},{3,1},{4,6},{5,7},{6,4},{7,5},{8,10},{9,11},{10,... | collective-permute-start | bytes 589832 | tf_op jit(solution)/shard_map/ppermute | solution.py:291
  232.2 41.0 %collective-permute-start.96 = (bf16[128,768]{1,0:T(8,128)(2,1)}, bf16[128,768]{1,0:T(8,128)(2,1)}, u32[]{:S(2)}, u32[]{:S(2)}) collective-permute-start(bf16[128,768]{1,0:T(8,128)(2,1)} %get-tuple-element.134.refs_0_), channel_id=1, source_target_pairs={{0,2},{1,3},{2,0},{3,1},{4,6},{5,7},{6,4},{7,5},{8,10},{9,11},{10,... | collective-permute-start | bytes 589832 | tf_op jit(solution)/shard_map/ppermute | solution.py:291
  236.5 19.0 %collective-permute-start.46 = (bf16[128,768]{1,0:T(8,128)(2,1)}, bf16[128,768]{1,0:T(8,128)(2,1)}, u32[]{:S(2)}, u32[]{:S(2)}) collective-permute-start(bf16[128,768]{1,0:T(8,128)(2,1)} %get-tuple-element.147.refs_0_), channel_id=1, source_target_pairs={{0,1},{1,0},{2,3},{3,2},{4,5},{5,4},{6,7},{7,6},{8,9},{9,8},{10,11... | collective-permute-start | bytes 589832 | tf_op jit(solution)/shard_map/ppermute | solution.py:291
  273.2 75.4 %collective-permute-start.86 = (bf16[16,768]{1,0:T(8,128)(2,1)}, bf16[16,768]{1,0:T(8,128)(2,1)}, u32[]{:S(2)}, u32[]{:S(2)}) collective-permute-start(bf16[16,768]{1,0:T(8,128)(2,1)} %broadcast_select_fusion.6), channel_id=1, source_target_pairs={{0,2},{1,3},{2,0},{3,1},{4,6},{5,7},{6,4},{7,5},{8,10},{9,11},{10,... | collective-permute-start | bytes 73736 | tf_op jit(solution)/shard_map/ppermute | solution.py:291
  273.7 19.0 %collective-permute-start.97 = (bf16[128,768]{1,0:T(8,128)(2,1)}, bf16[128,768]{1,0:T(8,128)(2,1)}, u32[]{:S(2)}, u32[]{:S(2)}) collective-permute-start(bf16[128,768]{1,0:T(8,128)(2,1)} %collective-permute-done.96), channel_id=1, source_target_pairs={{0,1},{1,0},{2,3},{3,2},{4,5},{5,4},{6,7},{7,6},{8,9},{9,8},{10,11... | collective-permute-start | bytes 589832 | tf_op jit(solution)/shard_map/ppermute | solution.py:291
  273.7 17.3 %collective-permute-start.64 = (bf16[256,576]{1,0:T(8,128)(2,1)}, bf16[256,576]{1,0:T(8,128)(2,1)}, u32[]{:S(2)}, u32[]{:S(2)}) collective-permute-start(bf16[256,576]{1,0:T(8,128)(2,1)} %get-tuple-element.204), channel_id=1, source_target_pairs={{0,2},{1,3},{2,0},{3,1},{4,6},{5,7},{6,4},{7,5},{8,10},{9,11},{10,... | collective-permute-start | bytes 884744 | tf_op jit(solution)/shard_map/ppermute | solution.py:291
  291.0 35.1 %collective-permute-start.120 = (bf16[4,96,768]{2,1,0:T(8,128)(2,1)}, bf16[4,96,768]{2,1,0:T(8,128)(2,1)}, u32[]{:S(2)}, u32[]{:S(2)}) collective-permute-start(bf16[4,96,768]{2,1,0:T(8,128)(2,1)} %dynamic-slice_bitcast_fusion.2), channel_id=1, source_target_pairs={{0,4},{4,0},{8,12},{12,8},{16,20},{20,16},{24,28},{28,24},{1,5},{5... | collective-permute-start | bytes 1769480 | tf_op jit(solution)/shard_map/ppermute | solution.py:291
  292.7 18.3 %collective-permute-start.110 = (bf16[4,96,192]{2,1,0:T(8,128)(2,1)}, bf16[4,96,192]{2,1,0:T(8,128)(2,1)}, u32[]{:S(2)}, u32[]{:S(2)}) collective-permute-start(bf16[4,96,192]{2,1,0:T(8,128)(2,1)} %bitcast.498), channel_id=1, source_target_pairs={{0,4},{4,0},{8,12},{12,8},{16,20},{20,16},{24,28},{28,24},{1,5},{5... | collective-permute-start | bytes 442376 | tf_op jit(solution)/shard_map/ppermute | solution.py:291
  318.7 22.3 %all-to-all-start = ((bf16[8,16,576]{2,1,0:T(8,128)(2,1)}), bf16[8,16,576]{2,1,0:T(8,128)(2,1)S(1)}, u32[]{:S(2)}, u32[]{:S(2)}) async-start(bf16[8,16,576]{2,1,0:T(8,128)(2,1)} %bitcast.53), calls=%async_computation | async-start | bytes 327680 | tf_op jit(solution)/shard_map/all_to_all | solution.py:320
  323.4 16.7 %collective-permute-start.132 = (bf16[4,96,768]{2,1,0:T(8,128)(2,1)}, bf16[4,96,768]{2,1,0:T(8,128)(2,1)S(1)}, u32[]{:S(2)}, u32[]{:S(2)}) collective-permute-start(bf16[4,96,768]{2,1,0:T(8,128)(2,1)} %dynamic-slice_bitcast_fusion), channel_id=1, source_target_pairs={{0,4},{4,0},{8,12},{12,8},{16,20},{20,16},{24,28},{28,24},{1,5},{5... | collective-permute-start | bytes 1769480 | tf_op jit(solution)/shard_map/ppermute | solution.py:291
  326.1 41.6 %collective-permute-start.76 = (bf16[8,2,24,768]{3,2,1,0:T(8,128)(2,1)}, bf16[8,2,24,768]{3,2,1,0:T(8,128)(2,1)}, u32[]{:S(2)}, u32[]{:S(2)}) collective-permute-start(bf16[8,2,24,768]{3,2,1,0:T(8,128)(2,1)} %fusion.13), channel_id=1, source_target_pairs={{0,1},{1,0},{2,3},{3,2},{4,5},{5,4},{6,7},{7,6},{8,9},{9,8},{10,11... | collective-permute-start | bytes 1769480 | tf_op jit(solution)/shard_map/ppermute | solution.py:291
  363.0 65.1 %collective-permute-start.125 = (bf16[256,768]{1,0:T(8,128)(2,1)}, bf16[256,768]{1,0:T(8,128)(2,1)S(1)}, u32[]{:S(2)}, u32[]{:S(2)}) collective-permute-start(bf16[256,768]{1,0:T(8,128)(2,1)} %copy-done.175), channel_id=1, source_target_pairs={{0,2},{1,3},{2,0},{3,1},{4,6},{5,7},{6,4},{7,5},{8,10},{9,11},{10,... | collective-permute-start | bytes 1179656 | tf_op jit(solution)/shard_map/ppermute | solution.py:291
  395.7 26.5 %collective-permute-start.123 = (bf16[128,768]{1,0:T(8,128)(2,1)S(1)}, bf16[128,768]{1,0:T(8,128)(2,1)S(1)}, u32[]{:S(2)}, u32[]{:S(2)}) collective-permute-start(bf16[128,768]{1,0:T(8,128)(2,1)S(1)} %get-tuple-element.162.refs_0_), channel_id=1, source_target_pairs={{0,2},{1,3},{2,0},{3,1},{4,6},{5,7},{6,4},{7,5},{8,10},{9,11},{10,... | collective-permute-start | bytes 589832 | tf_op jit(solution)/shard_map/ppermute | solution.py:291
  422.1 27.1 %collective-permute-start.113 = (bf16[128,768]{1,0:T(8,128)(2,1)S(1)}, bf16[128,768]{1,0:T(8,128)(2,1)S(1)}, u32[]{:S(2)}, u32[]{:S(2)}) collective-permute-start(bf16[128,768]{1,0:T(8,128)(2,1)S(1)} %copy-done.70), channel_id=1, source_target_pairs={{0,2},{1,3},{2,0},{3,1},{4,6},{5,7},{6,4},{7,5},{8,10},{9,11},{10,... | collective-permute-start | bytes 589832 | tf_op jit(solution)/shard_map/ppermute | solution.py:291
  431.1 20.7 %collective-permute-start.58 = (bf16[256,768]{1,0:T(8,128)(2,1)S(1)}, bf16[256,768]{1,0:T(8,128)(2,1)S(1)}, u32[]{:S(2)}, u32[]{:S(2)}) collective-permute-start(bf16[256,768]{1,0:T(8,128)(2,1)S(1)} %get-tuple-element.194), channel_id=1, source_target_pairs={{0,2},{1,3},{2,0},{3,1},{4,6},{5,7},{6,4},{7,5},{8,10},{9,11},{10,... | collective-permute-start | bytes 1179656 | tf_op jit(solution)/shard_map/ppermute | solution.py:291
  447.7 38.4 %collective-permute-start.103 = (bf16[256,192]{1,0:T(8,128)(2,1)}, bf16[256,192]{1,0:T(8,128)(2,1)}, u32[]{:S(2)}, u32[]{:S(2)}) collective-permute-start(bf16[256,192]{1,0:T(8,128)(2,1)} %get-tuple-element.212), channel_id=1, source_target_pairs={{0,2},{1,3},{2,0},{3,1},{4,6},{5,7},{6,4},{7,5},{8,10},{9,11},{10,... | collective-permute-start | bytes 294920 | tf_op jit(solution)/shard_map/ppermute | solution.py:291
  449.2 54.7 %collective-permute-start.92 = (bf16[128,768]{1,0:T(8,128)(2,1)}, bf16[128,768]{1,0:T(8,128)(2,1)}, u32[]{:S(2)}, u32[]{:S(2)}) collective-permute-start(bf16[128,768]{1,0:T(8,128)(2,1)} %collective-permute-done.91), channel_id=1, source_target_pairs={{0,1},{1,0},{2,3},{3,2},{4,5},{5,4},{6,7},{7,6},{8,9},{9,8},{10,11... | collective-permute-start | bytes 589832 | tf_op jit(solution)/shard_map/ppermute | solution.py:291
  453.2 19.4 %collective-permute-start.101 = (bf16[128,768]{1,0:T(8,128)(2,1)}, bf16[128,768]{1,0:T(8,128)(2,1)}, u32[]{:S(2)}, u32[]{:S(2)}) collective-permute-start(bf16[128,768]{1,0:T(8,128)(2,1)} %get-tuple-element.168.refs_0_), channel_id=1, source_target_pairs={{0,2},{1,3},{2,0},{3,1},{4,6},{5,7},{6,4},{7,5},{8,10},{9,11},{10,... | collective-permute-start | bytes 589832 | tf_op jit(solution)/shard_map/ppermute | solution.py:291
  472.5 56.2 %collective-permute-start.126 = (bf16[4,96,768]{2,1,0:T(8,128)(2,1)}, bf16[4,96,768]{2,1,0:T(8,128)(2,1)}, u32[]{:S(2)}, u32[]{:S(2)}) collective-permute-start(bf16[4,96,768]{2,1,0:T(8,128)(2,1)} %dynamic-slice_bitcast_fusion.1), channel_id=1, source_target_pairs={{0,4},{4,0},{8,12},{12,8},{16,20},{20,16},{24,28},{28,24},{1,5},{5... | collective-permute-start | bytes 1769480 | tf_op jit(solution)/shard_map/ppermute | solution.py:291
  486.5 54.4 %collective-permute-start.115 = (bf16[4,96,768]{2,1,0:T(8,128)(2,1)}, bf16[4,96,768]{2,1,0:T(8,128)(2,1)}, u32[]{:S(2)}, u32[]{:S(2)}) collective-permute-start(bf16[4,96,768]{2,1,0:T(8,128)(2,1)} %dynamic-slice_bitcast_fusion.3), channel_id=1, source_target_pairs={{0,4},{4,0},{8,12},{12,8},{16,20},{20,16},{24,28},{28,24},{1,5},{5... | collective-permute-start | bytes 1769480 | tf_op jit(solution)/shard_map/ppermute | solution.py:291
  504.0 62.3 %collective-permute-start.71 = (bf16[8,2,24,768]{3,2,1,0:T(8,128)(2,1)}, bf16[8,2,24,768]{3,2,1,0:T(8,128)(2,1)}, u32[]{:S(2)}, u32[]{:S(2)}) collective-permute-start(bf16[8,2,24,768]{3,2,1,0:T(8,128)(2,1)} %fusion.17), channel_id=1, source_target_pairs={{0,1},{1,0},{2,3},{3,2},{4,5},{5,4},{6,7},{7,6},{8,9},{9,8},{10,11... | collective-permute-start | bytes 1769480 | tf_op jit(solution)/shard_map/ppermute | solution.py:291
  521.4 21.8 %all-to-all-start.1 = ((bf16[8,16,576]{2,1,0:T(8,128)(2,1)}), bf16[8,16,576]{2,1,0:T(8,128)(2,1)}, u32[]{:S(2)}, u32[]{:S(2)}) async-start(bf16[8,16,576]{2,1,0:T(8,128)(2,1)} %bitcast.491), calls=%async_computation.1 | async-start | bytes 327680 | tf_op jit(solution)/shard_map/all_to_all | solution.py:320
  525.8 37.8 %collective-permute-start.93 = (bf16[4,96,576]{2,1,0:T(8,128)(2,1)}, bf16[4,96,576]{2,1,0:T(8,128)(2,1)}, u32[]{:S(2)}, u32[]{:S(2)}) collective-permute-start(bf16[4,96,576]{2,1,0:T(8,128)(2,1)} %dynamic-slice_bitcast_fusion.9), channel_id=1, source_target_pairs={{0,4},{4,0},{8,12},{12,8},{16,20},{20,16},{24,28},{28,24},{1,5},{5... | collective-permute-start | bytes 1327112 | tf_op jit(solution)/shard_map/ppermute | solution.py:291
  538.9 21.7 %collective-permute-start.127 = (bf16[2,96,768]{2,1,0:T(8,128)(2,1)}, bf16[2,96,768]{2,1,0:T(8,128)(2,1)}, u32[]{:S(2)}, u32[]{:S(2)}) collective-permute-start(bf16[2,96,768]{2,1,0:T(8,128)(2,1)} %dynamic-slice_bitcast_fusion.11), channel_id=1, source_target_pairs={{0,8},{4,12},{8,0},{12,4},{16,24},{20,28},{24,16},{28,20},{1,9},{5... | collective-permute-start | bytes 884744 | tf_op jit(solution)/shard_map/ppermute | solution.py:291
  554.4 27.1 %collective-permute-start.116 = (bf16[2,96,768]{2,1,0:T(8,128)(2,1)S(1)}, bf16[2,96,768]{2,1,0:T(8,128)(2,1)S(1)}, u32[]{:S(2)}, u32[]{:S(2)}) collective-permute-start(bf16[2,96,768]{2,1,0:T(8,128)(2,1)S(1)} %copy-done.237), channel_id=1, source_target_pairs={{0,8},{4,12},{8,0},{12,4},{16,24},{20,28},{24,16},{28,20},{1,9},{5... | collective-permute-start | bytes 884744 | tf_op jit(solution)/shard_map/ppermute | solution.py:291
  555.2 19.9 %collective-permute-start.56 = (f32[64,768]{1,0:T(8,128)S(1)}, f32[64,768]{1,0:T(8,128)S(1)}, u32[]{:S(2)}, u32[]{:S(2)}) collective-permute-start(f32[64,768]{1,0:T(8,128)S(1)} %get-tuple-element.301), channel_id=1, source_target_pairs={{0,2},{1,3},{2,0},{3,1},{4,6},{5,7},{6,4},{7,5},{8,10},{9,11},{10,... | collective-permute-start | bytes 589832 | tf_op jit(solution)/shard_map/ppermute | solution.py:291
  569.1 20.9 %collective-permute-start.94 = (bf16[2,96,576]{2,1,0:T(8,128)(2,1)S(1)}, bf16[2,96,576]{2,1,0:T(8,128)(2,1)S(1)}, u32[]{:S(2)}, u32[]{:S(2)}) collective-permute-start(bf16[2,96,576]{2,1,0:T(8,128)(2,1)S(1)} %dynamic-slice_bitcast_fusion.17), channel_id=1, source_target_pairs={{0,8},{4,12},{8,0},{12,4},{16,24},{20,28},{24,16},{28,20},{1,9},{5... | collective-permute-start | bytes 663560 | tf_op jit(solution)/shard_map/ppermute | solution.py:291
  571.0 29.6 %collective-permute-start.72 = (bf16[8,24,768]{2,1,0:T(8,128)(2,1)S(1)}, bf16[8,24,768]{2,1,0:T(8,128)(2,1)S(1)}, u32[]{:S(2)}, u32[]{:S(2)}) collective-permute-start(bf16[8,24,768]{2,1,0:T(8,128)(2,1)S(1)} %dynamic-slice_bitcast_fusion.15), channel_id=1, source_target_pairs={{0,2},{1,3},{2,0},{3,1},{4,6},{5,7},{6,4},{7,5},{8,10},{9,11},{10,... | collective-permute-start | bytes 884744 | tf_op jit(solution)/shard_map/ppermute | solution.py:291
  (359 other events, 2127.7 us)
